TPU v7x, 128 devices: a whole 4x4x4 slice. The times are simulated.
128 devices in a mesh: section: 2 (over x_hi), dp: 16 (over x_lo, y, core), node: 4 (over z).
Axes of the slice: x: 4 (x_hi: 2, x_lo: 2; x = x_hi * 2 + x_lo), y: 4, z: 4, core: 2. Of those that a mesh axis runs over, the one named last changes fastest.
Arguments:
- hidden_in: bfloat16 [2, 16384, 8192], P('section', ('dp', 'node')), may hold values from -8 to 8
- norm_gain: float32 [2, 8192], P('section'), may hold values from 0.1 to 1.9
- weight_codes: int32 [2, 8192, 1024], P('section', 'node'), may hold values from -127 to 127
- block_scales: float32 [2, 32, 1024], P('section', 'node'), may hold values from 7e-05 to 0.0003
- value_grad: bfloat16 [2, 16384, 1024], P('section', ('dp', 'node')), may hold values from -16 to 16
Outputs:
- passed_values: bfloat16 [2, 16384, 1024], P('section', ('dp', 'node'))
- input_grad: bfloat16 [2, 16384, 8192], P('section', ('dp', 'node'))
- weight_grad: bfloat16 [2, 8192, 1024], P('section', ('dp', 'node'))
All inputs are finite; a program needn't handle non-finite values.
Results may differ from a plain program's by a relative error of at most 0.025.
Values may be sent and summed in bfloat16 or wider, within the bound.
A program may use at most 192 MiB of HBM per device.

v0:
```python
import jax
import jax.numpy as jnp
from jax import lax
from jax.sharding import PartitionSpec as P


def from_behind(value, axis, steps):
    count = lax.axis_size(axis)
    pairs = [(source, (source + steps) % count) for source in range(count)]
    return lax.ppermute(value, axis, pairs)


def dequantize(codes, scales):
    rows = codes.shape[0]
    cols = codes.shape[1]
    groups = scales.shape[0]
    scaled = codes.astype(jnp.float32).reshape(groups, rows // groups, cols) * scales[:, None, :]
    return scaled.reshape(rows, cols).astype(jnp.bfloat16)


def on_device(hidden_in, norm_gain, weight_codes, block_scales, value_grad):
    inputs_raw = hidden_in[0]
    inputs = inputs_raw.astype(jnp.float32)
    gain_vec = norm_gain[0]
    cotan = value_grad[0]
    tokens_section = inputs_raw.shape[0] * lax.axis_size("dp") * lax.axis_size("node")
    factor = float(tokens_section) ** (-0.5)
    local_weights = dequantize(weight_codes[0], block_scales[0])
    inv_rms = lax.rsqrt(jnp.mean(inputs * inputs, axis=-1, keepdims=True) + 1e-05)
    normed = (inputs * inv_rms * gain_vec).astype(jnp.bfloat16)
    weights = lax.all_gather(local_weights, "node", axis=0, tiled=True)
    values = jnp.dot(normed, weights, preferred_element_type=jnp.float32).astype(jnp.bfloat16)
    normed_grad = lax.dot_general(
        cotan, weights, (((1,), (1,)), ((), ())), preferred_element_type=jnp.float32
    )
    scaled_grad = gain_vec * normed_grad
    inner = jnp.mean(inputs * scaled_grad, axis=-1, keepdims=True)
    input_grad = (inv_rms * scaled_grad - inputs * inv_rms * inv_rms * inv_rms * inner).astype(
        jnp.bfloat16
    )
    full_term = (
        lax.dot_general(normed, cotan, (((0,), (0,)), ((), ())), preferred_element_type=jnp.float32)
        * factor
    )
    group_sum = lax.psum_scatter(
        full_term.astype(jnp.bfloat16), "dp", scatter_dimension=0, tiled=True
    ).astype(jnp.float32)
    group_sum = group_sum.astype(jnp.bfloat16).astype(jnp.float32)
    weight_grad = lax.psum_scatter(
        group_sum.astype(jnp.bfloat16), "node", scatter_dimension=0, tiled=True
    )
    passed_values = from_behind(values[None], "section", 1)
    return (passed_values, input_grad[None], weight_grad[None])


def solution(mesh):
    return jax.shard_map(
        on_device,
        mesh=mesh,
        in_specs=(
            P("section", ("dp", "node"), None),
            P("section", None),
            P("section", "node", None),
            P("section", "node", None),
            P("section", ("dp", "node"), None),
        ),
        out_specs=(
            P("section", ("dp", "node"), None),
            P("section", ("dp", "node"), None),
            P("section", ("dp", "node"), None),
        ),
        check_vma=False,
    )
```

profile of v0, /device:TPU:1, one launch (start us, length us, event | category | flops | bytes accessed | tf_op | source)
XLA Modules:
  0.0 334.6 jit_solution(17236399747450410148)
XLA Ops:
  7.2 0.0 copy-start
  7.2 0.0 all-gather.2.cloned.1.call-start
  7.2 6.8 %fusion.15 = bf16[2048,1024]{1,0:T(8,128)(2,1)} fusion(s32[1,2048,1024]{2,1,0:T(8,128)} %param.7, f32[8,1024]{1,0:T(8,128)} %bitcast.60), kind=kLoop, calls=%fused_computation.20 | loop fusion | flops 6291456 | bytes 12615680 | tf_op jit(solution)/shard_map/convert_element_type | solution.py:18
  14.0 0.0 copy-start.3
  14.0 0.0 all-gather.2.cloned.1.call-update
  14.0 0.0 reduce-scatter.3.cloned.1.call-start
  14.1 6.4 %copy.8 = bf16[1,256,8192]{1,2,0:T(8,128)(2,1)} copy(bf16[1,256,8192]{2,1,0:T(8,128)(2,1)} %param.5) | data formatting | bytes 8388608 | tf_op args[0]
  20.4 151.1 %all-gather.2.cloned.1.call-done = bf16[8192,1024]{1,0:T(8,128)(2,1)} async-done(((bf16[2048,1024]{1,0:T(8,128)(2,1)}), bf16[8192,1024]{1,0:T(8,128)(2,1)}) %all-gather.2.cloned.1.call-update) | async-done | bytes 16777232 | tf_op jit(solution)/shard_map/all_gather | solution.py:31
  171.5 0.0 copy-done
  171.5 0.0 copy-done.3
  171.5 0.0 copy-start.2
  171.5 11.7 %fusion.12 = (f32[256]{0:T(256)S(1)}, f32[256]{0:T(256)S(1)}, f32[256,8192]{0,1:T(8,128)}) fusion(bf16[1,256,8192]{1,2,0:T(8,128)(2,1)} %copy.8, bf16[8192,1024]{1,0:T(8,128)(2,1)} %all-gather.2.cloned.1.call-done, bf16[1,256,1024]{2,1,0:T(8,128)(2,1)S(1)} %copy-done, f32[8192]{0:T(1024)S(1)} %bitcast.62), kind=kOutput, calls=%fused_computation.16 | convolution fusion | flops 4307550208 | bytes 29919232 | tf_op jit(solution)/shard_map/dot_general | solution.py:33
  183.3 0.0 copy-done.2
  183.3 9.0 %multiply_convert_fusion = bf16[8192,1024]{1,0:T(8,128)(2,1)} fusion(bf16[1,256,8192]{1,2,0:T(8,128)(2,1)S(1)} %copy-done.2, f32[8192]{0:T(1024)S(1)} %bitcast.63, f32[256]{0:T(256)S(1)} %add_rsqrt_fusion, bf16[1,256,1024]{2,1,0:T(8,128)(2,1)S(1)} %copy-done), kind=kOutput, calls=%fused_computation | convolution fusion | flops 4320133120 | bytes 21529600 | tf_op jit(solution)/shard_map/dot_general | solution.py:42
  192.3 0.0 reduce-scatter.3.cloned.1.call-update
  192.3 0.0 reduce-scatter.5.cloned.1.call-start
  192.3 11.7 %fusion.28 = bf16[1,256,1024]{2,1,0:T(8,128)(2,1)S(1)} fusion(bf16[8192,1024]{1,0:T(8,128)(2,1)} %all-gather.2.cloned.1.call-done, bf16[1,256,8192]{1,2,0:T(8,128)(2,1)} %copy.8, f32[8192]{0:T(1024)S(1)} %bitcast.64, f32[256]{0:T(256)S(1)} %add_rsqrt_fusion), kind=kOutput, calls=%fused_computation.29 | convolution fusion | flops 4303618048 | bytes 21529600 | tf_op jit(solution)/shard_map/dot_general | solution.py:32
  204.0 2.8 collective-permute-start
  206.8 92.5 %reduce-scatter.3.cloned.1.call-done = bf16[512,1024]{1,0:T(8,128)(2,1)} async-done(((bf16[8192,1024]{1,0:T(8,128)(2,1)}), bf16[512,1024]{1,0:T(8,128)(2,1)}) %reduce-scatter.3.cloned.1.call-update) | async-done | bytes 1048592 | tf_op jit(solution)/shard_map/reduce_scatter | solution.py:45
  299.2 0.0 reduce-scatter.5.cloned.1.call-update
  299.3 0.0 copy-start.1
  299.3 7.1 %fusion.18 = bf16[1,256,8192]{1,2,0:T(8,128)(2,1)} fusion(bf16[1,256,8192]{1,2,0:T(8,128)(2,1)} %copy.8, f32[256,8192]{0,1:T(8,128)} %get-tuple-element.8, f32[256]{0:T(256)S(1)} %broadcast_multiply_fusion, f32[256]{0:T(256)S(1)} %add_rsqrt_fusion), kind=kLoop, calls=%fused_computation.22 | loop fusion | flops 16777216 | bytes 16779264 | tf_op jit(solution)/shard_map/broadcast_in_dim | solution.py:53
  306.4 6.3 %copy.9 = bf16[1,256,8192]{2,1,0:T(8,128)(2,1)} copy(bf16[1,256,8192]{1,2,0:T(8,128)(2,1)} %fusion.18) | data formatting | bytes 8388608
  312.7 0.0 collective-permute-done
  312.7 14.6 %reduce-scatter.5.cloned.1.call-done = bf16[128,1024]{1,0:T(8,128)(2,1)} async-done(((bf16[512,1024]{1,0:T(8,128)(2,1)}), bf16[128,1024]{1,0:T(8,128)(2,1)}) %reduce-scatter.5.cloned.1.call-update) | async-done | bytes 262160 | tf_op jit(solution)/shard_map/reduce_scatter | solution.py:49
  327.3 0.8 copy.11
  328.1 0.0 copy-done.1
  (2 shorter events, 0.0 us)
Async XLA Ops:
  7.2 164.4 %copy-start = (bf16[1,256,1024]{2,1,0:T(8,128)(2,1)S(1)}, bf16[1,256,1024]{2,1,0:T(8,128)(2,1)}, u32[]{:S(2)}) copy-start(bf16[1,256,1024]{2,1,0:T(8,128)(2,1)} %param.9) | copy-start | bytes 1572868
  7.2 164.4 %all-gather.2.cloned.1.call-start = ((), (), s32[]{:S(2)}) async-start(), calls=%async_computation.2 | async-start | bytes 20971520 | tf_op jit(solution)/shard_map/all_gather | solution.py:31
  14.0 157.6 %copy-start.3 = (f32[1,8192]{1,0:T(1,128)S(1)}, f32[1,8192]{1,0:T(1,128)}, u32[]{:S(2)}) copy-start(f32[1,8192]{1,0:T(1,128)} %param.6) | copy-start | bytes 98308
  14.0 285.2 %reduce-scatter.3.cloned.1.call-start = ((), (), s32[]{:S(2)}) async-start(), calls=%async_computation.3 | async-start | bytes 17825792 | tf_op jit(solution)/shard_map/reduce_scatter | solution.py:45
  171.5 11.7 %copy-start.2 = (bf16[1,256,8192]{1,2,0:T(8,128)(2,1)S(1)}, bf16[1,256,8192]{1,2,0:T(8,128)(2,1)}, u32[]{:S(2)}) copy-start(bf16[1,256,8192]{1,2,0:T(8,128)(2,1)} %copy.8) | copy-start | bytes 12582916
  192.3 135.0 %reduce-scatter.5.cloned.1.call-start = ((), (), s32[]{:S(2)}) async-start(), calls=%async_computation.4 | async-start | bytes 1310720 | tf_op jit(solution)/shard_map/reduce_scatter | solution.py:49
  204.0 108.7 %collective-permute-start = (bf16[1,256,1024]{2,1,0:T(8,128)(2,1)S(1)}, bf16[1,256,1024]{2,1,0:T(8,128)(2,1)S(1)}, u32[]{:S(2)}, u32[]{:S(2)}) collective-permute-start(bf16[1,256,1024]{2,1,0:T(8,128)(2,1)S(1)} %fusion.28), channel_id=1, source_target_pairs={{0,64},{64,0},{1,65},{65,1},{2,66},{66,2},{3,67},{67,3},{4,68},{68... | collective-permute-start | bytes 1572872 | tf_op jit(solution)/shard_map/ppermute | solution.py:10
  299.3 28.8 %copy-start.1 = (bf16[1,256,1024]{2,1,0:T(8,128)(2,1)S(1)}, bf16[1,256,1024]{2,1,0:T(8,128)(2,1)}, u32[]{:S(2)}) copy-start(bf16[1,256,1024]{2,1,0:T(8,128)(2,1)} %param.9) | copy-start | bytes 1572868
Sparse Core Ops, SparseCore 0:
  14.1 157.3 all-gather.1
  192.4 106.7 reduce-scatter.2
  302.2 25.0 reduce-scatter.4
where the time goes:
time: 336 us; the launch traced here: 335 us
  waiting for transfers between devices  258 us (77%)
  matrix products  32.3 us (10%)
  other arithmetic  13.9 us (4%)
  between operations  13.8 us (4%)
  local copies, waits for them, and re-layouts  13.5 us (4%)
    all_gather x1, waiting for transfers between devices, on_device(): weights = lax.all_gather(local_weights, 'node', axis=0, tiled=True)  151 us
    reduce_scatter x1, waiting for transfers between devices, on_device(): lax.psum_scatter(full_term.astype(jnp.bfloat16), 'dp', scatter_dimension=...  92.5 us
    reduce_scatter x1, waiting for transfers between devices, on_device(): lax.psum_scatter(group_sum.astype(jnp.bfloat16), 'node', scatter_dimensio...  14.6 us
    unnamed x11, local copies, waits for them, and re-layouts  13.5 us
    dot_general x1, matrix products, on_device(): lax.dot_general(cotan, weights, (((1,), (1,)), ((), ())), preferred_eleme...  11.7 us
    dot_general x1, matrix products, on_device(): jnp.dot(normed, weights, preferred_element_type=jnp.float32)  11.7 us
    dot_general x1, matrix products, on_device(): lax.dot_general(normed, cotan, (((0,), (0,)), ((), ())), preferred_elemen...  8.97 us
    broadcast_in_dim x1, other arithmetic, on_device(): return (passed_values, input_grad[None], weight_grad[None])  7.12 us
  transfers between devices with their start and end apart: 4, of which 3 were waited for; matrix products, arithmetic and copies ran while one was open for 9% of the time, Pallas kernels for 0%

commit v1 on v0

v1 whole, which is shorter than its diff:
```python
import functools

import jax
import jax.numpy as jnp
from jax import lax
from jax.experimental import pallas as pl
from jax.experimental.pallas import tpu as pltpu
from jax.sharding import PartitionSpec as P

MESH = pl.DeviceIdType.MESH
BF16, F32 = jnp.bfloat16, jnp.float32
D, KV, TOK, NZ, NY = 8192, 1024, 256, 4, 4
SHARD = D // NZ
NB = 4
KB = KV // NB
BLK = 512
NBLK = D // BLK
FACTOR = 2.0 ** -7


def kernel(h_ref, gain_ref, codes_ref, scales_ref, cot_ref, pass_ref, ig_ref, wg_ref,
           hv, hs, cv, ct, nv, wall, cod, ng, part, y1, y2, xr, zr, vst, wgv, gv, sv, inv, cdv,
           l_sem, cod_sem, hs_s, hs_r, ct_s, ct_r, z_s, z_r, xw_s, xw_r, sw_s, sw_r,
           y1_s, y1_r, y2_s, y2_r, xr_s, xr_r, zr_s, zr_r, v_s, v_r, o_sem):
    sec, i, z = lax.axis_index("section"), lax.axis_index("dp"), lax.axis_index("node")
    x, y, c = i // 8, (i // 2) % 4, i % 2

    def dev(xx, yy, zz, cc, ss=None):
        return (sec if ss is None else ss, xx * 8 + yy * 2 + cc, zz)

    zp, zm, z2 = (z + 1) % 4, (z + 3) % 4, (z + 2) % 4
    yp, ym, yo = (y + 1) % 4, (y + 3) % 4, (y + 2) % 4
    d_sib, d_x = dev(x, y, z, 1 - c), dev(1 - x, y, z, c)
    d_yp, d_ym = dev(x, yp, z, c), dev(x, ym, z, c)
    d_z = [None, dev(x, y, zp, c), dev(x, y, z2, c), dev(x, y, zm, c)]
    d_sec = dev(x, y, z, c, 1 - sec)

    def remote(src, dst, s, r, device):
        return pltpu.make_async_remote_copy(src_ref=src, dst_ref=dst, send_sem=s, recv_sem=r,
                                            device_id=device, device_id_type=MESH)

    def load_h(b):
        return pltpu.make_async_copy(h_ref.at[0, :, pl.ds(pl.multiple_of(b * BLK, BLK), BLK)], hv.at[b], l_sem.at[b])

    def load_codes(kb):
        return pltpu.make_async_copy(codes_ref.at[0, :, pl.ds(kb * KB, KB)], cod.at[kb % 2], cod_sem.at[kb])

    cp_g = pltpu.make_async_copy(gain_ref, gv, l_sem.at[NBLK])
    cp_s = pltpu.make_async_copy(scales_ref.at[0], sv, l_sem.at[NBLK + 1])
    cp_c = pltpu.make_async_copy(cot_ref.at[0], cv, l_sem.at[NBLK + 2])
    cp_s.start()
    load_codes(0).start()
    load_codes(1).start()
    cp_c.start()
    cp_g.start()

    @pl.loop(0, NBLK)
    def _(b):
        load_h(b).start()

    barrier = pltpu.get_barrier_semaphore()
    for target in (d_sib, d_x, d_yp, d_ym, d_z[1], d_z[2], d_z[3], d_sec):
        pl.semaphore_signal(barrier, inc=1, device_id=target, device_id_type=MESH)
    pl.semaphore_wait(barrier, 8)

    def send_h(e):
        col = pl.multiple_of(e * (2 * BLK) + (1 - c) * BLK, BLK)
        return remote(h_ref.at[0, :, pl.ds(col, BLK)], hs.at[e], hs_s.at[e], hs_r.at[e], d_sib)

    @pl.loop(0, 8)
    def _(e):
        send_h(e).start()

    r0 = pl.multiple_of(c * 1024 + x * 256, 256)
    q0 = pl.multiple_of(c * 1024 + x * 768, 256)

    def z_copy(kb, k):
        if k == 0:
            ref = wall.at[kb, z, pl.ds(r0, 768)]
            return remote(ref, ref, z_s.at[kb, 0], z_r.at[kb, 0], d_z[1])
        if k == 1:
            ref = wall.at[kb, z, pl.ds(r0, 768)]
            return remote(ref, ref, z_s.at[kb, 1], z_r.at[kb, 1], d_z[3])
        if k == 2:
            ref = wall.at[kb, zm, pl.ds(r0, 384)]
            return remote(ref, ref, z_s.at[kb, 2], z_r.at[kb, 2], d_z[1])
        ref = wall.at[kb, zp, pl.ds(r0 + 384, 384)]
        return remote(ref, ref, z_s.at[kb, 3], z_r.at[kb, 3], d_z[3])

    shards = (zm, zp, z2)

    def x_copy(kb, k):
        ref = wall.at[kb, shards[k], pl.ds(q0, 256)]
        return remote(ref, ref, xw_s.at[kb, k], xw_r.at[kb, k], d_x)

    def sib_copy(kb, k):
        if k < 3:
            ref = wall.at[kb, shards[k], pl.ds(r0, 768)]
        else:
            ref = wall.at[kb, shards[k - 3], pl.ds(pl.multiple_of(c * 1024 + (1 - x) * 768, 256), 256)]
        return remote(ref, ref, sw_s.at[kb, k], sw_r.at[kb, k], d_sib)

    def dequant(kb):
        load_codes(kb).wait()

        @pl.loop(0, SHARD // 256)
        def _(g):
            rows = pl.ds(pl.multiple_of(g * 256, 256), 256)
            scale = sv[pl.ds(g, 1), kb * KB:(kb + 1) * KB]
            wall[kb, z, rows, :] = (cod[kb % 2, rows, :].astype(F32) * scale).astype(BF16)

        if kb + 2 < NB:
            load_codes(kb + 2).start()
        z_copy(kb, 0).start()
        z_copy(kb, 1).start()

    cp_s.wait()
    dequant(0)
    dequant(1)

    @pl.loop(0, NBLK)
    def _(b):
        load_h(b).wait()

    def squares(b, acc):
        v = hv[b].astype(F32)
        v = v * v
        return acc + v[:, 0:128] + v[:, 128:256] + v[:, 256:384] + v[:, 384:512]

    acc = lax.fori_loop(0, NBLK, squares, jnp.zeros((TOK, 128), F32))
    inv[...] = jnp.broadcast_to(lax.rsqrt(jnp.sum(acc, axis=1, keepdims=True) * (1.0 / D) + 1e-05), (TOK, 128))

    cp_c.wait()
    for q in range(4):
        scaled = cv[:, q * 256:(q + 1) * 256].astype(F32) * inv[:, 0:1]
        ct[0, q * 256:(q + 1) * 256, :] = jnp.transpose(scaled).astype(BF16)
    send_ct = remote(ct.at[0], ct.at[1], ct_s.at[0], ct_r.at[0], d_sib)
    send_ct.start()

    cp_g.wait()

    @pl.loop(0, NBLK)
    def _(b):
        g = gv[0:1, pl.ds(pl.multiple_of(b * BLK, BLK), BLK)]
        nv[b] = (hv[b].astype(F32) * inv[:, 0:1] * g).astype(BF16)

    @pl.loop(0, 8)
    def _(e):
        send_h(e).wait_recv()

    send_ct.wait_recv()

    def term(xx, yy):
        own = hv.at[xx * 8 + yy * 2 + c]
        other = hs.at[xx * 4 + yy]

        @pl.loop(0, 4)
        def _(q):
            rows = pl.ds(pl.multiple_of(q * 256, 256), 256)
            t = jnp.dot(ct[0, rows, :], own[...], preferred_element_type=F32)
            t = t + jnp.dot(ct[1, rows, :], other[...], preferred_element_type=F32)
            part[xx, yy, q] = (t * FACTOR).astype(BF16)

    def unit(u):
        n, q = u // 4, u % 4
        return (x + 1 + n) % 2, q

    def y1_copy(u, k):
        xx, q = unit(u)
        return remote(part.at[xx, yo, q, pl.ds(k * 128, 128)], y1.at[u, k], y1_s.at[u, k], y1_r.at[u, k],
                      (d_yp, d_ym)[k])

    def y2_copy(u, k):
        xx, q = unit(u)
        return remote(part.at[xx, (yp, ym)[k], q], y2.at[u, k], y2_s.at[u, k], y2_r.at[u, k], (d_yp, d_ym)[k])

    def xr_copy(q):
        return remote(part.at[1 - x, y, q], xr.at[q], xr_s.at[q], xr_r.at[q], d_x)

    def zr_copy(q, m):
        cols = pl.ds(pl.multiple_of(((z + m) % 4) * 128, 128), 128)
        return remote(part.at[x, y, q, :, cols], zr.at[q, m - 1], zr_s.at[q, m - 1], zr_r.at[q, m - 1], d_z[m])

    @pl.loop(0, 2)
    def _(n):
        term((x + 1 + n) % 2, yo)

        @pl.loop(0, 4)
        def _(q):
            y1_copy(n * 4 + q, 0).start()
            y1_copy(n * 4 + q, 1).start()

    @pl.loop(0, 2)
    def _(n):
        term((x + 1 + n) % 2, yp)
        term((x + 1 + n) % 2, ym)

    @pl.loop(0, 2)
    def _(n):
        term((x + 1 + n) % 2, y)

    def grad_a(lo, hi):
        @pl.loop(lo, hi)
        def _(u):
            xx, q = unit(u)
            y1_copy(u, 0).wait_recv()
            part[xx, yp, q, 0:128, :] = (part[xx, yp, q, 0:128, :].astype(F32) + y1[u, 0].astype(F32)).astype(BF16)
            y2_copy(u, 0).start()
            y1_copy(u, 1).wait_recv()
            part[xx, ym, q, 128:256, :] = (part[xx, ym, q, 128:256, :].astype(F32) + y1[u, 1].astype(F32)).astype(BF16)
            y2_copy(u, 1).start()

    def grad_b0(lo, hi):
        @pl.loop(lo, hi)
        def _(q):
            y2_copy(q, 0).wait_recv()
            y2_copy(q, 1).wait_recv()
            part[1 - x, y, q] = (part[1 - x, y, q].astype(F32) + y2[q, 0].astype(F32)
                                 + y2[q, 1].astype(F32)).astype(BF16)
            xr_copy(q).start()

    def grad_b1(lo, hi):
        @pl.loop(lo, hi)
        def _(q):
            xr_copy(q).wait_recv()
            y2_copy(4 + q, 0).wait_recv()
            y2_copy(4 + q, 1).wait_recv()
            part[x, y, q] = (part[x, y, q].astype(F32) + y2[4 + q, 0].astype(F32) + y2[4 + q, 1].astype(F32)
                             + xr[q].astype(F32)).astype(BF16)
            for m in (1, 2, 3):
                zr_copy(q, m).start()

    d0 = pl.multiple_of(i * 512 + z * 128, 128)

    def grad_c(q):
        for m in (1, 2, 3):
            zr_copy(q, m).wait_recv()
        own = part[x, y, q, :, pl.ds(pl.multiple_of(z * 128, 128), 128)].astype(F32)
        total = own + zr[q, 0].astype(F32) + zr[q, 1].astype(F32) + zr[q, 2].astype(F32)
        total = total * gv[0:1, pl.ds(d0, 128)]
        wgv[:, q * 256:(q + 1) * 256] = jnp.transpose(total).astype(BF16)

    def w_a(kb):
        z_copy(kb, 0).wait_recv()
        z_copy(kb, 2).start()
        x_copy(kb, 0).start()
        sib_copy(kb, 0).start()
        z_copy(kb, 1).wait_recv()
        z_copy(kb, 3).start()
        x_copy(kb, 1).start()
        sib_copy(kb, 1).start()

    def w_b(kb):
        z_copy(kb, 2).wait_recv()
        z_copy(kb, 3).wait_recv()
        x_copy(kb, 2).start()
        sib_copy(kb, 2).start()

    def w_c(kb):
        for k in range(3):
            x_copy(kb, k).wait_recv()
            sib_copy(kb, 3 + k).start()

    def pass_copy(kb):
        return remote(vst.at[kb], pass_ref.at[0, :, pl.ds(kb * KB, KB)], v_s.at[kb], v_r.at[kb], d_sec)

    def out_copy(b):
        return pltpu.make_async_copy(nv.at[b], ig_ref.at[0, :, pl.ds(pl.multiple_of(b * BLK, BLK), BLK)], o_sem.at[b])

    def w_d(kb):
        for k in range(6):
            sib_copy(kb, k).wait_recv()
        cols = slice(kb * KB, (kb + 1) * KB)
        last = kb == NB - 1

        def weight(b):
            return wall[kb, b // 4, pl.ds(pl.multiple_of((b % 4) * BLK, BLK), BLK), :]

        def grad_of(b):
            return lax.dot_general(cv[:, cols], weight(b), (((1,), (1,)), ((), ())), preferred_element_type=F32)

        def step(b, acc):
            w = weight(b)
            if not last:
                t = grad_of(b)
                if kb == 0:
                    ng[b] = t
                else:
                    ng[b] = ng[b] + t
            return acc + jnp.dot(nv[b], w, preferred_element_type=F32)

        vals = lax.fori_loop(0, NBLK, step, jnp.zeros((TOK, KB), F32))
        vst[kb] = vals.astype(BF16)
        pass_copy(kb).start()
        prod = vals * cv[:, cols].astype(F32)
        prod = prod[:, 0:128] + prod[:, 128:256]
        if kb == 0:
            cdv[...] = prod
        else:
            cdv[...] = cdv[...] + prod
        if last:
            iv = inv[:, 0:1]
            coef = iv * iv * (jnp.sum(cdv[...], axis=1, keepdims=True) * (1.0 / D))

            @pl.loop(0, NBLK)
            def _(b):
                g = gv[0:1, pl.ds(pl.multiple_of(b * BLK, BLK), BLK)]
                t = ng[b] + grad_of(b)
                nv[b] = (iv * g * t - hv[b].astype(F32) * coef).astype(BF16)
                out_copy(b).start()

    w_a(0)
    grad_a(0, 4)
    w_a(1)
    dequant(2)
    w_b(0)
    w_c(0)
    grad_a(4, 8)
    w_d(0)
    w_a(2)
    dequant(3)
    w_b(1)
    w_c(1)
    grad_b0(0, 1)
    w_d(1)
    w_a(3)
    grad_b0(1, 3)
    w_b(2)
    w_c(2)
    w_d(2)
    w_b(3)
    w_c(3)
    w_d(3)
    grad_b0(3, 4)
    grad_b1(0, 2)
    grad_c(0)
    grad_b1(2, 3)
    grad_c(1)
    grad_b1(3, 4)
    grad_c(2)
    grad_c(3)
    cp_w = pltpu.make_async_copy(wgv, wg_ref.at[0], l_sem.at[NBLK + 3])
    cp_w.start()

    @pl.loop(0, 8)
    def _(e):
        send_h(e).wait_send()
        for k in range(2):
            y1_copy(e, k).wait_send()
            y2_copy(e, k).wait_send()

    send_ct.wait_send()

    @pl.loop(0, 4)
    def _(q):
        xr_copy(q).wait_send()
        for m in (1, 2, 3):
            zr_copy(q, m).wait_send()

    for kb in range(NB):
        for k in range(4):
            z_copy(kb, k).wait_send()
        for k in range(3):
            x_copy(kb, k).wait_send()
        for k in range(6):
            sib_copy(kb, k).wait_send()
        pass_copy(kb).wait()

    @pl.loop(0, NBLK)
    def _(b):
        out_copy(b).wait()

    cp_w.wait()


def on_device(hidden_in, norm_gain, weight_codes, block_scales, value_grad):
    dma, any_ = pltpu.SemaphoreType.DMA, pl.BlockSpec(memory_space=pl.ANY)
    v = pltpu.VMEM
    return pl.pallas_call(
        kernel,
        out_shape=(
            jax.ShapeDtypeStruct((1, TOK, KV), BF16),
            jax.ShapeDtypeStruct((1, TOK, D), BF16),
            jax.ShapeDtypeStruct((1, 128, KV), BF16),
        ),
        in_specs=[any_] * 5,
        out_specs=[any_] * 3,
        scratch_shapes=[
            v((NBLK, TOK, BLK), BF16),
            v((8, TOK, BLK), BF16),
            v((TOK, KV), BF16),
            v((2, KV, TOK), BF16),
            v((NBLK, TOK, BLK), BF16),
            v((NB, NZ, SHARD, KB), BF16),
            v((2, SHARD, KB), jnp.int32),
            v((NBLK, TOK, BLK), F32),
            v((2, NY, 4, 256, BLK), BF16),
            v((8, 2, 128, BLK), BF16),
            v((8, 2, 256, BLK), BF16),
            v((4, 256, BLK), BF16),
            v((4, 3, 256, 128), BF16),
            v((NB, TOK, KB), BF16),
            v((128, KV), BF16),
            v((1, D), F32),
            v((8, KV), F32),
            v((TOK, 128), F32),
            v((TOK, 128), F32),
            dma((NBLK + 4,)), dma((NB,)),
            dma((8,)), dma((8,)), dma((1,)), dma((1,)),
            dma((NB, 4)), dma((NB, 4)), dma((NB, 3)), dma((NB, 3)), dma((NB, 6)), dma((NB, 6)),
            dma((8, 2)), dma((8, 2)), dma((8, 2)), dma((8, 2)),
            dma((4,)), dma((4,)), dma((4, 3)), dma((4, 3)), dma((NB,)), dma((NB,)), dma((NBLK,)),
        ],
        compiler_params=pltpu.CompilerParams(
            collective_id=0, has_side_effects=True, vmem_limit_bytes=63 * 2 ** 20),
        cost_estimate=pl.CostEstimate(flops=3 * 2 * TOK * D * KV, bytes_accessed=24 * 2 ** 20, transcendentals=TOK),
    )(hidden_in, norm_gain, weight_codes, block_scales, value_grad)


def solution(mesh):
    return jax.shard_map(
        on_device,
        mesh=mesh,
        in_specs=(
            P("section", ("dp", "node"), None),
            P("section", None),
            P("section", "node", None),
            P("section", "node", None),
            P("section", ("dp", "node"), None),
        ),
        out_specs=(
            P("section", ("dp", "node"), None),
            P("section", ("dp", "node"), None),
            P("section", ("dp", "node"), None),
        ),
        check_vma=False,
    )
```

time: 336 us -> 138 us (0.41)
  waiting for transfers between devices: 258 us -> 0 us
  Pallas kernels: 0 us -> 130 us
  matrix products: 32.3 us -> 0 us
  other arithmetic: 13.9 us -> 0 us
  between operations: 13.8 us -> 0.64 us
  local copies, waits for them, and re-layouts: 13.5 us -> 7.26 us
    all_gather x1 -> x0, waiting for transfers between devices: 151 us -> none  [on_device(): weights = lax.all_gather(local_weights, 'node', axis=0, tiled=True)]
    pallas_call x0 -> x1, Pallas kernels: none -> 130 us  [on_device(): pl.pallas_call(kernel, out_shape=(jax.ShapeDtypeStruct((1, TOK, KV), BF16...]
    reduce_scatter x2 -> x0, waiting for transfers between devices: 107 us -> none  [the longest x1 92.5 us: on_device(): lax.psum_scatter(full_term.astype(jnp.bfloat16), 'dp', scatter_dimension=...]
    dot_general x3 -> x0, matrix products: 32.3 us -> none  [the longest x1 11.7 us: on_device(): lax.dot_general(cotan, weights, (((1,), (1,)), ((), ())), preferred_eleme...]
    broadcast_in_dim x1 -> x0, other arithmetic: 7.12 us -> none  [on_device(): return (passed_values, input_grad[None], weight_grad[None])]
    convert_element_type x1 -> x0, other arithmetic: 6.76 us -> none  [dequantize(): return scaled.reshape(rows, cols).astype(jnp.bfloat16)]
    unnamed x11 -> x5, local copies, waits for them, and re-layouts: 13.5 us -> 7.26 us
  transfers between devices with their start and end apart: 4 -> 0, of which waited for: 3 -> 0; matrix products, arithmetic and copies ran while one was open for 9% -> 0% of each run, Pallas kernels for 0% -> 0%
where the time goes in v1:
time: 138 us
  Pallas kernels  130 us (94%)
  local copies, waits for them, and re-layouts  7.26 us (5%)
    pallas_call x1, Pallas kernels, on_device(): pl.pallas_call(kernel, out_shape=(jax.ShapeDtypeStruct((1, TOK, KV), BF16...  130 us
    unnamed x5, local copies, waits for them, and re-layouts  7.26 us

profile of v1, /device:TPU:1, one launch (start us, length us, event | category | flops | bytes accessed | tf_op | source)
XLA Modules:
  0.0 138.2 jit_solution(2356494624980592368)
XLA Ops:
  0.6 130.3 %shard_map.76 = (bf16[1,256,1024]{2,1,0:T(8,128)(2,1)}, bf16[1,256,8192]{2,1,0:T(8,128)(2,1)}, bf16[1,128,1024]{2,1,0:T(8,128)(2,1)}) custom-call(bf16[1,256,8192]{2,1,0:T(8,128)(2,1)} %h_ref.1, f32[1,8192]{1,0:T(1,128)} %gain_ref.1, s32[1,2048,1024]{2,1,0:T(8,128)} %codes_ref.1, f32[1,8,1024]{2,1,0:T(8,128)} %scales_ref.1, bf16[1,256,1024]{2,1,0:T(8,128)(2,1)} %cot_ref.1), custom_call_target="tpu_custom_call" | custom-call | flops 12884901888 | bytes 25165824 | tf_op jit(solution)/shard_map/pallas_call | solution.py:379
  131.0 1.9 %copy.11 = bf16[1,256,1024]{2,1,0:T(8,128)(2,1)} copy(bf16[1,256,1024]{2,1,0:T(8,128)(2,1)} %get-tuple-element.6) | data formatting | bytes 1048576
  132.8 0.0 copy-start
  132.8 4.7 %copy.12 = bf16[1,256,8192]{2,1,0:T(8,128)(2,1)} copy(bf16[1,256,8192]{2,1,0:T(8,128)(2,1)} %get-tuple-element.7) | data formatting | bytes 8388608
  137.5 0.0 copy-done
  137.5 0.7 copy.13
Async XLA Ops:
  132.8 4.7 %copy-start = (bf16[1,128,1024]{2,1,0:T(8,128)(2,1)S(1)}, bf16[1,128,1024]{2,1,0:T(8,128)(2,1)}, u32[]{:S(2)}) copy-start(bf16[1,128,1024]{2,1,0:T(8,128)(2,1)} %get-tuple-element.8) | copy-start | bytes 786436

commit v2 on v1

v2 whole, which is shorter than its diff:
```python
import functools

import jax
import jax.numpy as jnp
from jax import lax
from jax.experimental import pallas as pl
from jax.experimental.pallas import tpu as pltpu
from jax.sharding import PartitionSpec as P

MESH = pl.DeviceIdType.MESH
BF16, F32 = jnp.bfloat16, jnp.float32
D, KV, TOK, NZ, NY = 8192, 1024, 256, 4, 4
SHARD = D // NZ
NB = 4
KB = KV // NB
BLK = 512
NBLK = D // BLK
FACTOR = 2.0 ** -7
QR = 192
UN = 8
UR = KV // UN
PR = 1024 - 2 * QR


def kernel(h_ref, gain_ref, codes_ref, scales_ref, cot_ref, pass_ref, ig_ref, wg_ref,
           hv, cv, ct, nv, wall, cod, ng, part, y1, y2, xr, zr, vst, wgv, gv, sv, inv, cdv,
           l_sem, cod_sem, hs_s, hs_r, ct_s, ct_r, z_s, z_r, xw_s, xw_r, sw_s, sw_r,
           y1_s, y1_r, y2_s, y2_r, xr_s, xr_r, zr_s, zr_r, v_s, v_r, o_sem):
    sec, i, z = lax.axis_index("section"), lax.axis_index("dp"), lax.axis_index("node")
    x, y, c = i // 8, (i // 2) % 4, i % 2

    def dev(xx, yy, zz, cc, ss=None):
        return (sec if ss is None else ss, xx * 8 + yy * 2 + cc, zz)

    zp, zm, z2 = (z + 1) % 4, (z + 3) % 4, (z + 2) % 4
    yp, ym, yo = (y + 1) % 4, (y + 3) % 4, (y + 2) % 4
    d_sib, d_x = dev(x, y, z, 1 - c), dev(1 - x, y, z, c)
    d_yp, d_ym = dev(x, yp, z, c), dev(x, ym, z, c)
    d_z = [None, dev(x, y, zp, c), dev(x, y, z2, c), dev(x, y, zm, c)]
    d_sec = dev(x, y, z, c, 1 - sec)

    def remote(src, dst, s, r, device):
        return pltpu.make_async_remote_copy(src_ref=src, dst_ref=dst, send_sem=s, recv_sem=r,
                                            device_id=device, device_id_type=MESH)

    def load_h(e, k):
        bit = c if k == 0 else 1 - c
        col = pl.multiple_of(e * (2 * BLK) + bit * BLK, BLK)
        return pltpu.make_async_copy(h_ref.at[0, :, pl.ds(col, BLK)], hv.at[e, k], l_sem.at[e * 2 + k // 2])

    def load_codes(kb):
        return pltpu.make_async_copy(codes_ref.at[0, :, pl.ds(kb * KB, KB)], cod.at[kb % 2], cod_sem.at[kb])

    barrier = pltpu.get_barrier_semaphore()
    for target in (d_sib, d_x, d_yp, d_ym, d_z[1], d_z[2], d_z[3], d_sec):
        pl.semaphore_signal(barrier, inc=1, device_id=target, device_id_type=MESH)

    cp_g = pltpu.make_async_copy(gain_ref, gv, l_sem.at[NBLK])
    cp_s = pltpu.make_async_copy(scales_ref.at[0], sv, l_sem.at[NBLK + 1])
    cp_c = pltpu.make_async_copy(cot_ref.at[0], cv, l_sem.at[NBLK + 2])
    cp_s.start()
    load_codes(0).start()

    @pl.loop(0, 8)
    def _(e):
        load_h(e, 0).start()
        load_h(e, 2).start()

    cp_c.start()
    load_codes(1).start()
    cp_g.start()

    def send_h(e):
        col = pl.multiple_of(e * (2 * BLK) + (1 - c) * BLK, BLK)
        return remote(h_ref.at[0, :, pl.ds(col, BLK)], hv.at[e, 1], hs_s.at[e], hs_r.at[e], d_sib)

    base = c * 1024
    p0 = pl.multiple_of(base + QR, 32)
    q0 = pl.multiple_of(base + x * (QR + PR), 32)
    q1 = pl.multiple_of(base + (1 - x) * (QR + PR), 32)
    r0 = pl.multiple_of(base + x * QR, 32)

    def z_copy(kb, k):
        start, size = (q0, QR) if k < 4 else (p0, PR)
        if k % 4 < 2:
            ref = wall.at[kb, z, pl.ds(start, size)]
        elif k % 4 == 2:
            ref = wall.at[kb, zm, pl.ds(start, size // 2)]
        else:
            ref = wall.at[kb, zp, pl.ds(pl.multiple_of(start + size // 2, 16), size // 2)]
        return remote(ref, ref, z_s.at[kb, k], z_r.at[kb, k], d_z[1 if k % 2 == 0 else 3])

    shards = (zm, zp, z2)

    def x_copy(kb, k):
        ref = wall.at[kb, shards[k], pl.ds(q0, QR)]
        return remote(ref, ref, xw_s.at[kb, k], xw_r.at[kb, k], d_x)

    def sib_copy(kb, k):
        if k < 3:
            ref = wall.at[kb, shards[k], pl.ds(r0, PR + QR)]
        else:
            ref = wall.at[kb, shards[k - 3], pl.ds(q1, QR)]
        return remote(ref, ref, sw_s.at[kb, k], sw_r.at[kb, k], d_sib)

    def dequant(kb):
        load_codes(kb).wait()

        @pl.loop(0, SHARD // 256)
        def _(g):
            rows = pl.ds(pl.multiple_of(g * 256, 256), 256)
            scale = sv[pl.ds(g, 1), kb * KB:(kb + 1) * KB]
            wall[kb, z, rows, :] = (cod[kb % 2, rows, :].astype(F32) * scale).astype(BF16)

        if kb + 2 < NB:
            load_codes(kb + 2).start()

    def w_send(kb):
        for k in (0, 1, 4, 5):
            z_copy(kb, k).start()

    cp_s.wait()
    dequant(0)
    pl.semaphore_wait(barrier, 8)

    @pl.loop(0, 8)
    def _(e):
        send_h(e).start()

    w_send(0)

    @pl.loop(0, 8)
    def _(e):
        load_h(e, 0).wait()
        load_h(e, 2).wait()

    def squares(e, acc):
        for k in (0, 2):
            v = hv[e, k].astype(F32)
            v = v * v
            acc = acc + (v[:, 0:128] + v[:, 128:256]) + (v[:, 256:384] + v[:, 384:512])
        return acc

    acc = lax.fori_loop(0, 8, squares, jnp.zeros((TOK, 128), F32))
    inv[...] = jnp.broadcast_to(lax.rsqrt(jnp.sum(acc, axis=1, keepdims=True) * (1.0 / D) + 1e-05), (TOK, 128))

    cp_c.wait()
    for q in range(4):
        scaled = cv[:, q * 256:(q + 1) * 256].astype(F32) * inv[:, 0:1]
        ct[q * 256:(q + 1) * 256, 0:256] = jnp.transpose(scaled).astype(BF16)
    send_ct = remote(ct.at[:, pl.ds(0, 256)], ct.at[:, pl.ds(256, 256)], ct_s.at[0], ct_r.at[0], d_sib)
    send_ct.start()
    cp_g.wait()
    dequant(1)
    w_send(1)

    @pl.loop(0, 8)
    def _(e):
        send_h(e).wait_recv()

    send_ct.wait_recv()

    def term(xx, yy):
        both = hv[xx * 4 + yy, 0:2].reshape(2 * TOK, BLK)

        for lo in (0, 256):
            t = jnp.dot(ct[...], both[:, lo:lo + 256], preferred_element_type=F32)
            part[xx, yy, :, :, lo:lo + 256] = (t * FACTOR).astype(BF16).reshape(UN, UR, 256)

    def row(n):
        return (x + 1 + n) % 2

    def y1_copy(n, q, k):
        return remote(part.at[row(n), yo, q, pl.ds(k * (UR // 2), UR // 2)], y1.at[n, q, k],
                      y1_s.at[n, q, k], y1_r.at[n, q, k], (d_yp, d_ym)[k])

    def y2_copy(n, q, k):
        return remote(part.at[row(n), (yp, ym)[k], q], y2.at[n, q, k], y2_s.at[n, q, k], y2_r.at[n, q, k],
                      (d_yp, d_ym)[k])

    def xr_copy(q):
        return remote(part.at[1 - x, y, q], xr.at[q], xr_s.at[q], xr_r.at[q], d_x)

    def zr_copy(q, m):
        cols = pl.ds(pl.multiple_of(((z + m) % 4) * 128, 128), 128)
        return remote(part.at[x, y, q, :, cols], zr.at[q, m - 1], zr_s.at[q, m - 1], zr_r.at[q, m - 1], d_z[m])

    def y1_send(n):
        term(row(n), yo)

        @pl.loop(0, UN)
        def _(q):
            y1_copy(n, q, 0).start()
            y1_copy(n, q, 1).start()

    def terms(n):
        for yy in (yp, ym):
            term(row(n), yy)

    def grad_a(n, q, k):
        xx, yy = row(n), (yp, ym)[k]
        rows = slice(k * (UR // 2), (k + 1) * (UR // 2))
        y1_copy(n, q, k).wait_recv()
        part[xx, yy, q, rows, :] = (part[xx, yy, q, rows, :].astype(F32) + y1[n, q, k].astype(F32)).astype(BF16)
        y2_copy(n, q, k).start()

    def y_sum(n, q):
        y2_copy(n, q, 0).wait_recv()
        y2_copy(n, q, 1).wait_recv()
        return part[row(n), y, q].astype(F32) + y2[n, q, 0].astype(F32) + y2[n, q, 1].astype(F32)

    def grad_b0(q):
        part[1 - x, y, q] = y_sum(0, q).astype(BF16)
        xr_copy(q).start()

    def grad_b1(q):
        xr_copy(q).wait_recv()
        part[x, y, q] = (y_sum(1, q) + xr[q].astype(F32)).astype(BF16)
        for m in (1, 3, 2):
            zr_copy(q, m).start()

    d0 = pl.multiple_of(i * 512 + z * 128, 128)

    def grad_c(q):
        for m in (1, 2, 3):
            zr_copy(q, m).wait_recv()
        own = part[x, y, q, :, pl.ds(pl.multiple_of(z * 128, 128), 128)].astype(F32)
        total = own + zr[q, 0].astype(F32) + zr[q, 1].astype(F32) + zr[q, 2].astype(F32)
        total = total * gv[0:1, pl.ds(d0, 128)]
        wgv[:, q * UR:(q + 1) * UR] = jnp.transpose(total).astype(BF16)

    def w_q(kb, k):
        z_copy(kb, k).wait_recv()
        z_copy(kb, 2 + k).start()
        x_copy(kb, k).start()

    def w_p(kb, k):
        z_copy(kb, 4 + k).wait_recv()
        z_copy(kb, 6 + k).start()
        sib_copy(kb, k).start()

    def w_bq(kb):
        z_copy(kb, 2).wait_recv()
        z_copy(kb, 3).wait_recv()
        x_copy(kb, 2).start()

    def w_bp(kb):
        z_copy(kb, 6).wait_recv()
        z_copy(kb, 7).wait_recv()
        sib_copy(kb, 2).start()

    def w_c(kb, k):
        x_copy(kb, k).wait_recv()
        sib_copy(kb, 3 + k).start()

    def pass_copy(kb):
        return remote(vst.at[kb], pass_ref.at[0, :, pl.ds(kb * KB, KB)], v_s.at[kb], v_r.at[kb], d_sec)

    def out_copy(zz):
        return pltpu.make_async_copy(nv.at[zz], ig_ref.at[0, :, pl.ds(pl.multiple_of(zz * SHARD, SHARD), SHARD)],
                                     o_sem.at[zz])

    def h_block(zz, r):
        return hv[zz * 2 + r // 2, jnp.where(c == r % 2, 0, 2)].astype(F32)

    def gain_block(zz, r):
        return gv[0:1, pl.ds(pl.multiple_of(zz * SHARD + r * BLK, BLK), BLK)]

    def normalize():
        @pl.loop(0, NZ)
        def _(zz):
            for r in range(4):
                nv[zz, :, r * BLK:(r + 1) * BLK] = (h_block(zz, r) * inv[:, 0:1] * gain_block(zz, r)).astype(BF16)

    def grad_of(kb, zz, lo, size):
        return lax.dot_general(cv[:, kb * KB:(kb + 1) * KB], wall[kb, zz, lo:lo + size, :], (((1,), (1,)), ((), ())),
                               preferred_element_type=F32)

    def w_d(kb):
        for k in range(6):
            sib_copy(kb, k).wait_recv()
        cols = slice(kb * KB, (kb + 1) * KB)
        last = kb == NB - 1

        def step(zz, acc):
            if not last:
                for lo in (0, 1024):
                    t = grad_of(kb, zz, lo, 1024)
                    if kb == 0:
                        ng[zz, :, lo:lo + 1024] = t
                    else:
                        ng[zz, :, lo:lo + 1024] = ng[zz, :, lo:lo + 1024] + t
            return acc + jnp.dot(nv[zz], wall[kb, zz], preferred_element_type=F32)

        vals = lax.fori_loop(0, NZ, step, jnp.zeros((TOK, KB), F32))
        vst[kb] = vals.astype(BF16)
        pass_copy(kb).start()
        prod = vals * cv[:, cols].astype(F32)
        prod = prod[:, 0:128] + prod[:, 128:256]
        if kb == 0:
            cdv[...] = prod
        else:
            cdv[...] = cdv[...] + prod

    def w_e():
        kb = NB - 1
        iv = inv[:, 0:1]
        coef = iv * iv * (jnp.sum(cdv[...], axis=1, keepdims=True) * (1.0 / D))

        @pl.loop(0, NZ)
        def _(zz):
            for r in range(4):
                lanes = slice(r * BLK, (r + 1) * BLK)
                t = ng[zz, :, lanes] + grad_of(kb, zz, r * BLK, BLK)
                nv[zz, :, lanes] = (iv * gain_block(zz, r) * t - h_block(zz, r) * coef).astype(BF16)
            out_copy(zz).start()

    y1_send(0)
    y1_send(1)
    w_q(0, 0)
    w_q(0, 1)
    dequant(2)
    w_send(2)
    dequant(3)
    w_send(3)
    terms(0)
    w_q(1, 0)
    w_q(1, 1)
    w_p(0, 0)
    w_p(0, 1)
    w_c(0, 0)
    grad_a(0, 0, 0)
    grad_a(0, 0, 1)
    grad_a(0, 1, 0)
    grad_a(0, 1, 1)
    grad_a(0, 2, 0)
    grad_a(0, 2, 1)
    grad_a(0, 3, 0)
    grad_a(0, 3, 1)
    w_c(0, 1)
    grad_a(0, 4, 0)
    grad_a(0, 4, 1)
    terms(1)
    w_c(1, 0)
    grad_a(0, 5, 0)
    grad_a(0, 5, 1)
    grad_a(0, 6, 0)
    grad_a(0, 6, 1)
    term(row(0), y)
    grad_a(0, 7, 0)
    w_c(1, 1)
    grad_a(0, 7, 1)
    term(row(1), y)
    w_p(1, 0)
    w_p(1, 1)
    grad_a(1, 0, 0)
    grad_a(1, 0, 1)
    w_bq(0)
    normalize()
    grad_a(1, 1, 0)
    grad_a(1, 1, 1)
    grad_a(1, 2, 0)
    w_q(2, 0)
    w_q(2, 1)
    grad_a(1, 2, 1)
    grad_a(1, 3, 0)
    grad_a(1, 3, 1)
    w_c(0, 2)
    grad_a(1, 4, 0)
    grad_a(1, 4, 1)
    w_c(2, 0)
    grad_a(1, 5, 0)
    grad_a(1, 5, 1)
    grad_a(1, 6, 0)
    grad_a(1, 6, 1)
    w_c(2, 1)
    grad_a(1, 7, 0)
    w_p(2, 0)
    w_p(2, 1)
    grad_a(1, 7, 1)
    w_q(3, 0)
    w_q(3, 1)
    grad_b0(0)
    grad_b0(1)
    w_c(3, 0)
    w_c(3, 1)
    grad_b0(2)
    w_p(3, 0)
    w_p(3, 1)
    w_bq(1)
    grad_b0(3)
    w_bp(0)
    grad_b0(4)
    w_d(0)
    w_bq(2)
    w_bp(1)
    w_c(1, 2)
    grad_b0(5)
    grad_b0(6)
    w_d(1)
    w_bq(3)
    w_bp(2)
    grad_b0(7)
    grad_b1(0)
    w_bp(3)
    grad_b1(1)
    w_c(2, 2)
    grad_c(0)
    w_d(2)
    grad_b1(2)
    grad_b1(3)
    grad_c(1)
    grad_b1(4)
    grad_c(2)
    grad_c(3)
    grad_b1(5)
    w_c(3, 2)
    w_d(3)
    grad_b1(6)
    grad_c(4)
    w_e()
    grad_b1(7)
    grad_c(5)
    grad_c(6)
    grad_c(7)
    cp_w = pltpu.make_async_copy(wgv, wg_ref.at[0], l_sem.at[NBLK + 3])
    cp_w.start()

    @pl.loop(0, 8)
    def _(e):
        send_h(e).wait_send()

    send_ct.wait_send()

    @pl.loop(0, UN)
    def _(q):
        for n in range(2):
            for k in range(2):
                y1_copy(n, q, k).wait_send()
                y2_copy(n, q, k).wait_send()
        xr_copy(q).wait_send()
        for m in (1, 2, 3):
            zr_copy(q, m).wait_send()

    for kb in range(NB):
        for k in range(8):
            z_copy(kb, k).wait_send()
        for k in range(3):
            x_copy(kb, k).wait_send()
        for k in range(6):
            sib_copy(kb, k).wait_send()
        pass_copy(kb).wait()

    for zz in range(NZ):
        out_copy(zz).wait()

    cp_w.wait()


def hand_over(a_in, b_in, c_in, a_out, b_out, c_out, a_v, b_v, c_v, sem_in, sem_out):
    refs = [(a_in.at[0], a_v, a_out.at[0]), (c_in.at[0], c_v, c_out.at[0])]
    for k in range(8):
        rows = pl.ds(k * 32, 32)
        refs.append((b_in.at[0, rows], b_v.at[rows], b_out.at[0, rows]))
    first = [pltpu.make_async_copy(a, b, sem_in.at[k]) for k, (a, b, _) in enumerate(refs)]
    second = [pltpu.make_async_copy(b, d, sem_out.at[k]) for k, (_, b, d) in enumerate(refs)]
    for copy in first:
        copy.start()
    for one, two in zip(first, second):
        one.wait()
        two.start()
    for copy in second:
        copy.wait()


def on_device(hidden_in, norm_gain, weight_codes, block_scales, value_grad):
    dma, any_ = pltpu.SemaphoreType.DMA, pl.BlockSpec(memory_space=pl.ANY)
    v = pltpu.VMEM
    out = pl.pallas_call(
        kernel,
        out_shape=(
            jax.ShapeDtypeStruct((1, TOK, KV), BF16),
            jax.ShapeDtypeStruct((1, TOK, D), BF16),
            jax.ShapeDtypeStruct((1, 128, KV), BF16),
        ),
        in_specs=[any_] * 5,
        out_specs=[any_] * 3,
        scratch_shapes=[
            v((8, 3, TOK, BLK), BF16),
            v((TOK, KV), BF16),
            v((KV, 2 * TOK), BF16),
            v((NZ, TOK, SHARD), BF16),
            v((NB, NZ, SHARD, KB), BF16),
            v((2, SHARD, KB), jnp.int32),
            v((NZ, TOK, SHARD), F32),
            v((2, NY, UN, UR, BLK), BF16),
            v((2, UN, 2, UR // 2, BLK), BF16),
            v((2, UN, 2, UR, BLK), BF16),
            v((UN, UR, BLK), BF16),
            v((UN, 3, UR, 128), BF16),
            v((NB, TOK, KB), BF16),
            v((128, KV), BF16),
            v((1, D), F32),
            v((8, KV), F32),
            v((TOK, 128), F32),
            v((TOK, 128), F32),
            dma((NBLK + 4,)), dma((NB,)),
            dma((8,)), dma((8,)), dma((1,)), dma((1,)),
            dma((NB, 8)), dma((NB, 8)), dma((NB, 3)), dma((NB, 3)), dma((NB, 6)), dma((NB, 6)),
            dma((2, UN, 2)), dma((2, UN, 2)), dma((2, UN, 2)), dma((2, UN, 2)),
            dma((UN,)), dma((UN,)), dma((UN, 3)), dma((UN, 3)), dma((NB,)), dma((NB,)), dma((NZ,)),
        ],
        compiler_params=pltpu.CompilerParams(
            collective_id=0, has_side_effects=True, vmem_limit_bytes=63 * 2 ** 20),
        cost_estimate=pl.CostEstimate(flops=3 * 2 * TOK * D * KV, bytes_accessed=24 * 2 ** 20, transcendentals=TOK),
    )(hidden_in, norm_gain, weight_codes, block_scales, value_grad)
    return pl.pallas_call(
        hand_over,
        out_shape=tuple(jax.ShapeDtypeStruct(o.shape, o.dtype) for o in out),
        in_specs=[any_] * 3,
        out_specs=[any_] * 3,
        scratch_shapes=[v((TOK, KV), BF16), v((TOK, D), BF16), v((128, KV), BF16), dma((10,)), dma((10,))],
    )(*out)


def solution(mesh):
    return jax.shard_map(
        on_device,
        mesh=mesh,
        in_specs=(
            P("section", ("dp", "node"), None),
            P("section", None),
            P("section", "node", None),
            P("section", "node", None),
            P("section", ("dp", "node"), None),
        ),
        out_specs=(
            P("section", ("dp", "node"), None),
            P("section", ("dp", "node"), None),
            P("section", ("dp", "node"), None),
        ),
        check_vma=False,
    )
```

time: 138 us -> 96.7 us (0.70)
  Pallas kernels: 130 us -> 95.9 us
  local copies, waits for them, and re-layouts: 7.26 us -> 0 us
    pallas_call x1, Pallas kernels: 130 us -> 91.5 us  [on_device(): pl.pallas_call(kernel, out_shape=(jax.ShapeDtypeStruct((1, TOK, KV), BF16...]
    unnamed x5 -> x0, local copies, waits for them, and re-layouts: 7.26 us -> none
    pallas_call x0 -> x1, Pallas kernels: none -> 4.44 us  [on_device(): pl.pallas_call(hand_over, out_shape=tuple((jax.ShapeDtypeStruct(o.shape,...]
where the time goes in v2:
time: 96.7 us; the launch traced here: 96.6 us
  Pallas kernels  95.9 us (99%)
    pallas_call x1, Pallas kernels, on_device(): pl.pallas_call(kernel, out_shape=(jax.ShapeDtypeStruct((1, TOK, KV), BF16...  91.5 us
    pallas_call x1, Pallas kernels, on_device(): pl.pallas_call(hand_over, out_shape=tuple((jax.ShapeDtypeStruct(o.shape,...  4.44 us

profile of v2, /device:TPU:1, one launch (start us, length us, event | category | flops | bytes accessed | tf_op | source)
XLA Modules:
  0.0 96.6 jit_solution(15199696213053322938)
XLA Ops:
  0.6 91.5 %shard_map.76 = (bf16[1,256,1024]{2,1,0:T(8,128)(2,1)}, bf16[1,256,8192]{2,1,0:T(8,128)(2,1)}, bf16[1,128,1024]{2,1,0:T(8,128)(2,1)}) custom-call(bf16[1,256,8192]{2,1,0:T(8,128)(2,1)} %h_ref.1, f32[1,8192]{1,0:T(1,128)} %gain_ref.1, s32[1,2048,1024]{2,1,0:T(8,128)} %codes_ref.1, f32[1,8,1024]{2,1,0:T(8,128)} %scales_ref.1, bf16[1,256,1024]{2,1,0:T(8,128)(2,1)} %cot_ref.1), custom_call_target="tpu_custom_call" | custom-call | flops 12884901888 | bytes 25165824 | tf_op jit(solution)/shard_map/pallas_call | solution.py:479
  92.1 4.4 %shard_map.77 = (bf16[1,256,1024]{2,1,0:T(8,128)(2,1)}, bf16[1,256,8192]{2,1,0:T(8,128)(2,1)}, bf16[1,128,1024]{2,1,0:T(8,128)(2,1)}) custom-call(bf16[1,256,1024]{2,1,0:T(8,128)(2,1)} %get-tuple-element.6.a_in, bf16[1,256,8192]{2,1,0:T(8,128)(2,1)} %get-tuple-element.7.b_in, bf16[1,128,1024]{2,1,0:T(8,128)(2,1)} %get-tuple-element.8.c_in), custom_call_target="tpu_custom_call" | custom-call | tf_op jit(solution)/shard_map/pallas_call | solution.py:517

commit v3 on v2

v3 whole, which is shorter than its diff:
```python
import functools

import jax
import jax.numpy as jnp
from jax import lax
from jax.experimental import pallas as pl
from jax.experimental.pallas import tpu as pltpu
from jax.sharding import PartitionSpec as P

MESH = pl.DeviceIdType.MESH
BF16, F32 = jnp.bfloat16, jnp.float32
D, KV, TOK, NZ, NY = 8192, 1024, 256, 4, 4
SHARD = D // NZ
NB = 4
KB = KV // NB
BLK = 512
NBLK = D // BLK
FACTOR = 2.0 ** -7
QR = 208
ORDER = (2, 1, 3, 0)
PR = 1024 - 2 * QR


def kernel(h_ref, gain_ref, codes_ref, scales_ref, cot_ref, pass_ref, ig_ref, wg_ref,
           hv, cv, ct, nv, wall, cod, ng, hp, part, xr, zr, vst, wgv, gv, sv, inv, cdv,
           l_sem, cod_sem, own_sem, h_s, h_r, ct_s, ct_r, z_s, z_r, xw_s, xw_r, sw_s, sw_r,
           xr_s, xr_r, zr_s, zr_r, v_s, v_r, o_sem):
    sec, i, z = lax.axis_index("section"), lax.axis_index("dp"), lax.axis_index("node")
    x, y, c = i // 8, (i // 2) % 4, i % 2

    def dev(xx, yy, zz, cc, ss=None):
        return (sec if ss is None else ss, xx * 8 + yy * 2 + cc, zz)

    zp, zm, z2 = (z + 1) % 4, (z + 3) % 4, (z + 2) % 4
    yp, ym, yo = (y + 1) % 4, (y + 3) % 4, (y + 2) % 4
    d_sib, d_x = dev(x, y, z, 1 - c), dev(1 - x, y, z, c)
    d_y = {(t, k): dev(x, yy, z, c if k == 0 else 1 - c)
           for t, yy in enumerate((yp, ym, yo)) for k in range(2)}
    d_z = [None, dev(x, y, zp, c), dev(x, y, z2, c), dev(x, y, zm, c)]
    d_sec = dev(x, y, z, c, 1 - sec)

    def remote(src, dst, s, r, device):
        return pltpu.make_async_remote_copy(src_ref=src, dst_ref=dst, send_sem=s, recv_sem=r,
                                            device_id=device, device_id_type=MESH)

    def load_h(b):
        return pltpu.make_async_copy(h_ref.at[0, :, pl.ds(pl.multiple_of(b * BLK, BLK), BLK)], hv.at[b], l_sem.at[b])

    def load_codes(kb):
        return pltpu.make_async_copy(codes_ref.at[0, :, pl.ds(kb * KB, KB)], cod.at[kb % 2], cod_sem.at[kb])

    barrier = pltpu.get_barrier_semaphore()
    for target in (d_sib, d_x, *d_y.values(), d_z[1], d_z[2], d_z[3], d_sec):
        pl.semaphore_signal(barrier, inc=1, device_id=target, device_id_type=MESH)

    cp_g = pltpu.make_async_copy(gain_ref, gv, l_sem.at[NBLK])
    cp_s = pltpu.make_async_copy(scales_ref.at[0], sv, l_sem.at[NBLK + 1])
    cp_c = pltpu.make_async_copy(cot_ref.at[0], cv, l_sem.at[NBLK + 2])
    cp_s.start()
    load_codes(0).start()

    @pl.loop(0, NBLK)
    def _(b):
        load_h(b).start()

    cp_c.start()
    load_codes(1).start()
    cp_g.start()

    def h_copy(g, slot):
        xx = (x + 1 + g // 4) % 2
        yy = y if slot < 2 else (yp, ym, yo)[slot // 2 - 1]
        cc = c if slot % 2 == 0 else 1 - c
        lanes = pl.ds(pl.multiple_of(((z + ORDER[g % 4]) % 4) * 128, 128), 128)
        src, dst = hv.at[xx * 8 + yy * 2 + cc, :, lanes], hp.at[g, pl.ds(slot * TOK, TOK)]
        if slot == 0:
            return pltpu.make_async_copy(src, dst, own_sem.at[g])
        return remote(src, dst, h_s.at[g, slot], h_r.at[g, slot],
                      d_sib if slot == 1 else d_y[slot // 2 - 1, slot % 2])

    def h_send(g):
        for slot in (2, 4, 6, 3, 5, 7, 1, 0):
            h_copy(g, slot).start()

    def ct_copy(k):
        def cols(slot):
            return pl.ds(slot * TOK, TOK)

        if k < 3:
            src, dst, target = ct.at[:, cols(0)], ct.at[:, cols((2, 4, 1)[k])], (d_y[0, 0], d_y[1, 0], d_sib)[k]
        elif k < 5:
            rows = pl.ds((k - 3) * (KV // 2), KV // 2)
            src, dst, target = ct.at[rows, cols((2, 4)[k - 3])], ct.at[rows, cols(6)], d_y[k - 3, 0]
        else:
            slot = (2, 4, 6)[k - 5]
            src, dst, target = ct.at[:, cols(slot)], ct.at[:, cols(slot + 1)], d_sib
        return remote(src, dst, ct_s.at[k], ct_r.at[k], target)

    base = c * 1024
    p0 = pl.multiple_of(base + QR, 16)
    q0 = pl.multiple_of(base + x * (QR + PR), 16)
    q1 = pl.multiple_of(base + (1 - x) * (QR + PR), 16)
    r0 = pl.multiple_of(base + x * QR, 16)

    def z_copy(kb, k):
        start, size = (q0, QR) if k < 4 else (p0, PR)
        half = (size + 31) // 32 * 16
        if k % 4 < 2:
            ref = wall.at[kb, z, pl.ds(start, size)]
        elif k % 4 == 2:
            ref = wall.at[kb, zm, pl.ds(start, half)]
        else:
            ref = wall.at[kb, zp, pl.ds(pl.multiple_of(start + half, 16), size - half)]
        return remote(ref, ref, z_s.at[kb, k], z_r.at[kb, k], d_z[1 if k % 2 == 0 else 3])

    shards = (zm, zp, z2)

    def x_copy(kb, k):
        ref = wall.at[kb, shards[k], pl.ds(q0, QR)]
        return remote(ref, ref, xw_s.at[kb, k], xw_r.at[kb, k], d_x)

    def sib_copy(kb, k):
        if k < 3:
            ref = wall.at[kb, shards[k], pl.ds(r0, PR + QR)]
        else:
            ref = wall.at[kb, shards[k - 3], pl.ds(q1, QR)]
        return remote(ref, ref, sw_s.at[kb, k], sw_r.at[kb, k], d_sib)

    def dequant(kb):
        load_codes(kb).wait()

        @pl.loop(0, SHARD // 256)
        def _(g):
            rows = pl.ds(pl.multiple_of(g * 256, 256), 256)
            scale = sv[pl.ds(g, 1), kb * KB:(kb + 1) * KB]
            wall[kb, z, rows, :] = (cod[kb % 2, rows, :].astype(F32) * scale).astype(BF16)

        if kb + 2 < NB:
            load_codes(kb + 2).start()

    def q_send(kb):
        z_copy(kb, 0).start()
        z_copy(kb, 1).start()

    def p_send(kb):
        z_copy(kb, 4).start()
        z_copy(kb, 5).start()

    cp_s.wait()
    dequant(0)

    @pl.loop(0, NBLK)
    def _(b):
        load_h(b).wait()

    pl.semaphore_wait(barrier, 12)
    q_send(0)

    def scale_cot():
        def squares(b, acc):
            v = hv[b].astype(F32)
            v = v * v
            return acc + (v[:, 0:128] + v[:, 128:256]) + (v[:, 256:384] + v[:, 384:512])

        acc = lax.fori_loop(0, NBLK, squares, jnp.zeros((TOK, 128), F32))
        inv[...] = jnp.broadcast_to(lax.rsqrt(jnp.sum(acc, axis=1, keepdims=True) * (1.0 / D) + 1e-05), (TOK, 128))
        cp_c.wait()
        for q in range(4):
            scaled = cv[:, q * 256:(q + 1) * 256].astype(F32) * inv[:, 0:1]
            ct[q * 256:(q + 1) * 256, 0:TOK] = jnp.transpose(scaled).astype(BF16)
        for k in range(3):
            ct_copy(k).start()
        cp_g.wait()

    def ct_first(k):
        ct_copy(k).wait_recv()
        ct_copy(3 + k).start()
        ct_copy(5 + k).start()

    def ct_second():
        ct_copy(3).wait_recv()
        ct_copy(4).wait_recv()
        ct_copy(7).start()
        for k in (2, 5, 6, 7):
            ct_copy(k).wait_recv()

    def xr_copy(g):
        return remote(part.at[g], xr.at[g], xr_s.at[g], xr_r.at[g], d_x)

    def zr_copy(m):
        return remote(part.at[4 + ORDER.index(m)], zr.at[m - 1], zr_s.at[m - 1], zr_r.at[m - 1], d_z[m])

    def grad(g):
        h_copy(g, 0).wait()
        for slot in range(1, 8):
            h_copy(g, slot).wait_recv()
        if g >= 4:
            xr_copy(g - 4).wait_recv()

        @pl.loop(0, 4)
        def _(q):
            rows = pl.ds(pl.multiple_of(q * 256, 256), 256)
            t = jnp.dot(ct[rows, :], hp[g], preferred_element_type=F32) * FACTOR
            if g >= 4:
                t = t + xr[g - 4, rows, :].astype(F32)
            part[g, rows, :] = t.astype(BF16)

        if g < 4:
            xr_copy(g).start()
        elif ORDER[g - 4]:
            zr_copy(ORDER[g - 4]).start()

    d0 = pl.multiple_of(i * 512 + z * 128, 128)

    def grad_last():
        for m in (1, 2, 3):
            zr_copy(m).wait_recv()
        for q in range(4):
            rows = slice(q * 256, (q + 1) * 256)
            total = part[7, rows, :].astype(F32) + zr[0, rows, :].astype(F32)
            total = (total + zr[1, rows, :].astype(F32) + zr[2, rows, :].astype(F32)) * gv[0:1, pl.ds(d0, 128)]
            wgv[:, rows] = jnp.transpose(total).astype(BF16)

    def w_q(kb, k):
        z_copy(kb, k).wait_recv()
        z_copy(kb, 2 + k).start()
        x_copy(kb, k).start()

    def w_p(kb, k):
        z_copy(kb, 4 + k).wait_recv()
        z_copy(kb, 6 + k).start()
        sib_copy(kb, k).start()

    def w_bq(kb):
        z_copy(kb, 2).wait_recv()
        z_copy(kb, 3).wait_recv()
        x_copy(kb, 2).start()

    def w_bp(kb):
        z_copy(kb, 6).wait_recv()
        z_copy(kb, 7).wait_recv()
        sib_copy(kb, 2).start()

    def w_c(kb, k):
        x_copy(kb, k).wait_recv()
        sib_copy(kb, 3 + k).start()

    def pass_copy(kb):
        return remote(vst.at[kb], pass_ref.at[0, :, pl.ds(kb * KB, KB)], v_s.at[kb], v_r.at[kb], d_sec)

    def out_copy(zz):
        return pltpu.make_async_copy(nv.at[zz], ig_ref.at[0, :, pl.ds(pl.multiple_of(zz * SHARD, SHARD), SHARD)],
                                     o_sem.at[zz])

    def h_block(zz, r):
        return hv[zz * 4 + r].astype(F32)

    def gain_block(zz, r):
        return gv[0:1, pl.ds(pl.multiple_of(zz * SHARD + r * BLK, BLK), BLK)]

    def normalize():
        @pl.loop(0, NZ)
        def _(zz):
            for r in range(4):
                nv[zz, :, r * BLK:(r + 1) * BLK] = (h_block(zz, r) * inv[:, 0:1] * gain_block(zz, r)).astype(BF16)

    def grad_of(kb, zz, lo, size):
        return lax.dot_general(cv[:, kb * KB:(kb + 1) * KB], wall[kb, zz, lo:lo + size, :], (((1,), (1,)), ((), ())),
                               preferred_element_type=F32)

    def w_d(kb):
        for k in range(6):
            sib_copy(kb, k).wait_recv()
        cols = slice(kb * KB, (kb + 1) * KB)
        last = kb == NB - 1

        def step(zz, acc):
            if not last:
                for lo in (0, 1024):
                    t = grad_of(kb, zz, lo, 1024)
                    if kb == 0:
                        ng[zz, :, lo:lo + 1024] = t
                    else:
                        ng[zz, :, lo:lo + 1024] = ng[zz, :, lo:lo + 1024] + t
            return acc + jnp.dot(nv[zz], wall[kb, zz], preferred_element_type=F32)

        vals = lax.fori_loop(0, NZ, step, jnp.zeros((TOK, KB), F32))
        vst[kb] = vals.astype(BF16)
        pass_copy(kb).start()
        prod = vals * cv[:, cols].astype(F32)
        prod = prod[:, 0:128] + prod[:, 128:256]
        if kb == 0:
            cdv[...] = prod
        else:
            cdv[...] = cdv[...] + prod

    def w_e():
        kb = NB - 1
        iv = inv[:, 0:1]
        coef = iv * iv * (jnp.sum(cdv[...], axis=1, keepdims=True) * (1.0 / D))

        @pl.loop(0, NZ)
        def _(zz):
            for r in range(4):
                lanes = slice(r * BLK, (r + 1) * BLK)
                t = ng[zz, :, lanes] + grad_of(kb, zz, r * BLK, BLK)
                nv[zz, :, lanes] = (iv * gain_block(zz, r) * t - h_block(zz, r) * coef).astype(BF16)
            out_copy(zz).start()

    h_send(0)
    dequant(1)
    q_send(1)
    dequant(2)
    q_send(2)
    scale_cot()
    h_send(1)
    dequant(3)
    q_send(3)
    w_q(0, 1)
    p_send(0)
    w_q(0, 0)
    normalize()
    w_q(1, 1)
    w_q(1, 0)
    p_send(1)
    w_q(2, 1)
    w_q(2, 0)
    w_c(0, 1)
    w_q(3, 0)
    w_q(3, 1)
    w_c(0, 0)
    w_c(1, 1)
    w_c(1, 0)
    w_p(0, 0)
    ct_first(0)
    ct_first(1)
    w_p(0, 1)
    w_c(2, 1)
    h_send(2)
    w_bq(0)
    h_send(3)
    h_send(4)
    h_send(5)
    w_bq(1)
    h_send(6)
    w_c(2, 0)
    w_c(3, 0)
    w_c(3, 1)
    w_p(1, 0)
    w_p(1, 1)
    w_bq(2)
    p_send(2)
    p_send(3)
    w_c(0, 2)
    w_bq(3)
    h_send(7)
    ct_second()
    w_c(1, 2)
    grad(1)
    w_c(2, 2)
    w_bp(0)
    w_d(0)
    grad(0)
    w_c(3, 2)
    w_bp(1)
    grad(2)
    grad(3)
    w_p(2, 0)
    w_p(2, 1)
    w_d(1)
    w_p(3, 0)
    w_p(3, 1)
    grad(4)
    w_bp(2)
    grad(5)
    w_d(2)
    w_bp(3)
    grad(6)
    w_d(3)
    w_e()
    grad(7)
    grad_last()
    cp_w = pltpu.make_async_copy(wgv, wg_ref.at[0], l_sem.at[NBLK + 3])
    cp_w.start()

    for g in range(8):
        for slot in range(1, 8):
            h_copy(g, slot).wait_send()
    for k in range(8):
        ct_copy(k).wait_send()
    for g in range(4):
        xr_copy(g).wait_send()
    for m in (1, 2, 3):
        zr_copy(m).wait_send()

    for kb in range(NB):
        for k in range(8):
            z_copy(kb, k).wait_send()
        for k in range(3):
            x_copy(kb, k).wait_send()
        for k in range(6):
            sib_copy(kb, k).wait_send()
        pass_copy(kb).wait()

    for zz in range(NZ):
        out_copy(zz).wait()

    cp_w.wait()


def hand_over(a_in, b_in, c_in, a_out, b_out, c_out, a_v, b_v, c_v, sem_in, sem_out):
    refs = [(a_in.at[0], a_v, a_out.at[0]), (c_in.at[0], c_v, c_out.at[0])]
    for k in range(8):
        rows = pl.ds(k * 32, 32)
        refs.append((b_in.at[0, rows], b_v.at[rows], b_out.at[0, rows]))
    first = [pltpu.make_async_copy(a, b, sem_in.at[k]) for k, (a, b, _) in enumerate(refs)]
    second = [pltpu.make_async_copy(b, d, sem_out.at[k]) for k, (_, b, d) in enumerate(refs)]
    for copy in first:
        copy.start()
    for one, two in zip(first, second):
        one.wait()
        two.start()
    for copy in second:
        copy.wait()


def on_device(hidden_in, norm_gain, weight_codes, block_scales, value_grad):
    dma, any_ = pltpu.SemaphoreType.DMA, pl.BlockSpec(memory_space=pl.ANY)
    v = pltpu.VMEM
    out = pl.pallas_call(
        kernel,
        out_shape=(
            jax.ShapeDtypeStruct((1, TOK, KV), BF16),
            jax.ShapeDtypeStruct((1, TOK, D), BF16),
            jax.ShapeDtypeStruct((1, 128, KV), BF16),
        ),
        in_specs=[any_] * 5,
        out_specs=[any_] * 3,
        scratch_shapes=[
            v((NBLK, TOK, BLK), BF16),
            v((TOK, KV), BF16),
            v((KV, 8 * TOK), BF16),
            v((NZ, TOK, SHARD), BF16),
            v((NB, NZ, SHARD, KB), BF16),
            v((2, SHARD, KB), jnp.int32),
            v((NZ, TOK, SHARD), F32),
            v((8, 8 * TOK, 128), BF16),
            v((8, KV, 128), BF16),
            v((4, KV, 128), BF16),
            v((3, KV, 128), BF16),
            v((NB, TOK, KB), BF16),
            v((128, KV), BF16),
            v((1, D), F32),
            v((8, KV), F32),
            v((TOK, 128), F32),
            v((TOK, 128), F32),
            dma((NBLK + 4,)), dma((NB,)),
            dma((8,)), dma((8, 8)), dma((8, 8)), dma((8,)), dma((8,)),
            dma((NB, 8)), dma((NB, 8)), dma((NB, 3)), dma((NB, 3)), dma((NB, 6)), dma((NB, 6)),
            dma((4,)), dma((4,)), dma((3,)), dma((3,)), dma((NB,)), dma((NB,)), dma((NZ,)),
        ],
        compiler_params=pltpu.CompilerParams(
            collective_id=0, has_side_effects=True, vmem_limit_bytes=63 * 2 ** 20),
        cost_estimate=pl.CostEstimate(flops=3 * 2 * TOK * D * KV, bytes_accessed=24 * 2 ** 20, transcendentals=TOK),
    )(hidden_in, norm_gain, weight_codes, block_scales, value_grad)
    return pl.pallas_call(
        hand_over,
        out_shape=tuple(jax.ShapeDtypeStruct(o.shape, o.dtype) for o in out),
        in_specs=[any_] * 3,
        out_specs=[any_] * 3,
        scratch_shapes=[v((TOK, KV), BF16), v((TOK, D), BF16), v((128, KV), BF16), dma((10,)), dma((10,))],
    )(*out)


def solution(mesh):
    return jax.shard_map(
        on_device,
        mesh=mesh,
        in_specs=(
            P("section", ("dp", "node"), None),
            P("section", None),
            P("section", "node", None),
            P("section", "node", None),
            P("section", ("dp", "node"), None),
        ),
        out_specs=(
            P("section", ("dp", "node"), None),
            P("section", ("dp", "node"), None),
            P("section", ("dp", "node"), None),
        ),
        check_vma=False,
    )
```

time: 96.7 us -> 86.8 us (0.90)
  Pallas kernels: 95.9 us -> 86.1 us
    pallas_call x1, Pallas kernels: 91.5 us -> 81.6 us  [on_device(): pl.pallas_call(kernel, out_shape=(jax.ShapeDtypeStruct((1, TOK, KV), BF16...]
where the time goes in v3:
time: 86.8 us; the launch traced here: 86.7 us
  Pallas kernels  86.1 us (99%)
    pallas_call x1, Pallas kernels, on_device(): pl.pallas_call(kernel, out_shape=(jax.ShapeDtypeStruct((1, TOK, KV), BF16...  81.6 us
    pallas_call x1, Pallas kernels, on_device(): pl.pallas_call(hand_over, out_shape=tuple((jax.ShapeDtypeStruct(o.shape,...  4.44 us

profile of v3, /device:TPU:1, one launch (start us, length us, event | category | flops | bytes accessed | tf_op | source)
XLA Modules:
  0.0 86.7 jit_solution(10678552463640199667)
XLA Ops:
  0.6 81.6 %shard_map.76 = (bf16[1,256,1024]{2,1,0:T(8,128)(2,1)}, bf16[1,256,8192]{2,1,0:T(8,128)(2,1)}, bf16[1,128,1024]{2,1,0:T(8,128)(2,1)}) custom-call(bf16[1,256,8192]{2,1,0:T(8,128)(2,1)} %h_ref.1, f32[1,8192]{1,0:T(1,128)} %gain_ref.1, s32[1,2048,1024]{2,1,0:T(8,128)} %codes_ref.1, f32[1,8,1024]{2,1,0:T(8,128)} %scales_ref.1, bf16[1,256,1024]{2,1,0:T(8,128)(2,1)} %cot_ref.1), custom_call_target="tpu_custom_call" | custom-call | flops 12884901888 | bytes 25165824 | tf_op jit(solution)/shard_map/pallas_call | solution.py:430
  82.3 4.4 %shard_map.77 = (bf16[1,256,1024]{2,1,0:T(8,128)(2,1)}, bf16[1,256,8192]{2,1,0:T(8,128)(2,1)}, bf16[1,128,1024]{2,1,0:T(8,128)(2,1)}) custom-call(bf16[1,256,1024]{2,1,0:T(8,128)(2,1)} %get-tuple-element.6.a_in, bf16[1,256,8192]{2,1,0:T(8,128)(2,1)} %get-tuple-element.7.b_in, bf16[1,128,1024]{2,1,0:T(8,128)(2,1)} %get-tuple-element.8.c_in), custom_call_target="tpu_custom_call" | custom-call | tf_op jit(solution)/shard_map/pallas_call | solution.py:466

commit v4 on v3

v4 whole, which is shorter than its diff:
```python
import functools

import jax
import jax.numpy as jnp
from jax import lax
from jax.experimental import pallas as pl
from jax.experimental.pallas import tpu as pltpu
from jax.sharding import PartitionSpec as P

MESH = pl.DeviceIdType.MESH
BF16, F32 = jnp.bfloat16, jnp.float32
D, KV, TOK, NZ, NY = 8192, 1024, 256, 4, 4
SHARD = D // NZ
NB = 4
KB = KV // NB
BLK = 512
NBLK = D // BLK
FACTOR = 2.0 ** -7
QR = 208
ORDER = (2, 1, 3, 0)
PR = 1024 - 2 * QR


def kernel(h_ref, gain_ref, codes_ref, scales_ref, cot_ref, pass_ref, ig_ref, wg_ref,
           hv, cv, ct, nv, wall, cod, cq, ng, hp, part, xr, zr, zf, vst, gv, sv, inv, cdv,
           hl_sem, l_sem, cod_sem, own_sem, h_r, ct_r, z_r, xw_r, sw_r, xr_r, zr_r, v_r, send_sem):
    sec, i, z = lax.axis_index("section"), lax.axis_index("dp"), lax.axis_index("node")
    x, y, c = i // 8, (i // 2) % 4, i % 2

    def dev(xx, yy, zz, cc, ss=None):
        return (sec if ss is None else ss, xx * 8 + yy * 2 + cc, zz)

    zp, zm, z2 = (z + 1) % 4, (z + 3) % 4, (z + 2) % 4
    yp, ym, yo = (y + 1) % 4, (y + 3) % 4, (y + 2) % 4
    d_sib, d_x = dev(x, y, z, 1 - c), dev(1 - x, y, z, c)
    d_y = {(t, k): dev(x, yy, z, c if k == 0 else 1 - c)
           for t, yy in enumerate((yp, ym, yo)) for k in range(2)}
    d_z = [None, dev(x, y, zp, c), None, dev(x, y, zm, c)]
    d_sec = dev(x, y, z, c, 1 - sec)

    def remote(src, dst, s, r, device):
        return pltpu.make_async_remote_copy(src_ref=src, dst_ref=dst, send_sem=s, recv_sem=r,
                                            device_id=device, device_id_type=MESH)

    def load_h(b):
        return pltpu.make_async_copy(h_ref.at[0, :, pl.ds(pl.multiple_of(b * BLK, BLK), BLK)], hv.at[b], hl_sem.at[0])

    def wait_bytes(ref, sem):
        pltpu.make_async_copy(ref, ref, sem).wait()

    def load_codes(kb):
        return pltpu.make_async_copy(codes_ref.at[0, :, pl.ds(kb * KB, KB)], cod.at[kb % 2], cod_sem.at[kb])

    barrier = pltpu.get_barrier_semaphore()
    for target in (d_sib, d_x, *d_y.values(), d_z[1], d_z[3], d_sec):
        pl.semaphore_signal(barrier, inc=1, device_id=target, device_id_type=MESH)

    cp_g = pltpu.make_async_copy(gain_ref, gv, l_sem.at[0])
    cp_s = pltpu.make_async_copy(scales_ref.at[0], sv, l_sem.at[1])
    cp_c = pltpu.make_async_copy(cot_ref.at[0], cv, l_sem.at[2])
    quick = 4 * c + 3 * x
    cp_q = pltpu.make_async_copy(codes_ref.at[0, pl.ds(pl.multiple_of(quick * 256, 256), 256)], cq, l_sem.at[3])
    cp_q.start()
    cp_s.start()

    @pl.loop(0, NBLK)
    def _(b):
        load_h(b).start()

    cp_c.start()
    load_codes(0).start()
    load_codes(1).start()
    cp_g.start()

    def h_copy(g, slot):
        xx = (x + 1 + g // 4) % 2
        yy = y if slot < 2 else (yp, ym, yo)[slot // 2 - 1]
        cc = c if slot % 2 == 0 else 1 - c
        lanes = pl.ds(pl.multiple_of(((z + ORDER[g % 4]) % 4) * 128, 128), 128)
        src, dst = hv.at[xx * 8 + yy * 2 + cc, :, lanes], hp.at[g, pl.ds(slot * TOK, TOK)]
        if slot == 0:
            return pltpu.make_async_copy(src, dst, own_sem.at[0])
        return remote(src, dst, send_sem.at[0], h_r.at[g],
                      d_sib if slot == 1 else d_y[slot // 2 - 1, slot % 2])

    def h_send(g):
        for slot in (2, 4, 6, 3, 5, 7, 1):
            h_copy(g, slot).start()

    def ct_copy(k):
        def cols(slot):
            return pl.ds(slot * TOK, TOK)

        if k < 3:
            src, dst, target = ct.at[:, cols(0)], ct.at[:, cols((2, 4, 1)[k])], (d_y[0, 0], d_y[1, 0], d_sib)[k]
        elif k < 5:
            rows = pl.ds((k - 3) * (KV // 2), KV // 2)
            src, dst, target = ct.at[rows, cols((2, 4)[k - 3])], ct.at[rows, cols(6)], d_y[k - 3, 0]
        else:
            slot = (2, 4, 6)[k - 5]
            src, dst, target = ct.at[:, cols(slot)], ct.at[:, cols(slot + 1)], d_sib
        return remote(src, dst, send_sem.at[1], ct_r.at[(0, 1, 3, 2, 2, 3, 3, 3)[k]], target)

    base = c * 1024
    p0 = pl.multiple_of(base + QR, 16)
    q0 = pl.multiple_of(base + x * (QR + PR), 16)
    q1 = pl.multiple_of(base + (1 - x) * (QR + PR), 16)
    r0 = pl.multiple_of(base + x * QR, 16)

    def z_copy(kb, k):
        start, size = (q0, QR) if k < 4 else (p0, PR)
        half = (size + 31) // 32 * 16
        if k % 4 < 2:
            ref = wall.at[kb, z, pl.ds(start, size)]
        elif k % 4 == 2:
            ref = wall.at[kb, zm, pl.ds(start, half)]
        else:
            ref = wall.at[kb, zp, pl.ds(pl.multiple_of(start + half, 16), size - half)]
        return remote(ref, ref, send_sem.at[2], z_r.at[kb, (0, 1, 2, 2, 3, 4, 5, 5)[k]], d_z[1 if k % 2 == 0 else 3])

    shards = (zm, zp, z2)

    def x_copy(kb, k):
        ref = wall.at[kb, shards[k], pl.ds(q0, QR)]
        return remote(ref, ref, send_sem.at[3], xw_r.at[kb], d_x)

    def sib_copy(kb, k):
        if k < 3:
            ref = wall.at[kb, shards[k], pl.ds(r0, PR + QR)]
        else:
            ref = wall.at[kb, shards[k - 3], pl.ds(q1, QR)]
        return remote(ref, ref, send_sem.at[4], sw_r.at[kb], d_sib)

    def dequant(kb):
        load_codes(kb).wait()

        @pl.loop(1, SHARD // 256)
        def _(t):
            g = (quick + t) % (SHARD // 256)
            rows = pl.ds(pl.multiple_of(g * 256, 256), 256)
            scale = sv[pl.ds(g, 1), kb * KB:(kb + 1) * KB]
            wall[kb, z, rows, :] = (cod[kb % 2, rows, :].astype(F32) * scale).astype(BF16)

        if kb + 2 < NB:
            load_codes(kb + 2).start()

    def p_send(kb):
        z_copy(kb, 4).start()
        z_copy(kb, 5).start()

    cp_q.wait()
    cp_s.wait()
    for kb in range(NB):
        cols = slice(kb * KB, (kb + 1) * KB)
        wall[kb, z, pl.ds(pl.multiple_of(quick * 256, 256), 256), :] = (
            cq[:, cols].astype(F32) * sv[pl.ds(quick, 1), cols]).astype(BF16)
    pl.semaphore_wait(barrier, 11)
    for kb in range(NB):
        z_copy(kb, 0).start()
        z_copy(kb, 1).start()
    wait_bytes(hv, hl_sem.at[0])

    def scale_cot():
        def squares(b, acc):
            v = hv[b].astype(F32)
            v = v * v
            return acc + (v[:, 0:128] + v[:, 128:256]) + (v[:, 256:384] + v[:, 384:512])

        acc = lax.fori_loop(0, NBLK, squares, jnp.zeros((TOK, 128), F32))
        inv[...] = jnp.broadcast_to(lax.rsqrt(jnp.sum(acc, axis=1, keepdims=True) * (1.0 / D) + 1e-05), (TOK, 128))
        cp_c.wait()
        for q in range(4):
            scaled = cv[:, q * 256:(q + 1) * 256].astype(F32) * inv[:, 0:1]
            ct[q * 256:(q + 1) * 256, 0:TOK] = jnp.transpose(scaled).astype(BF16)
        for k in range(3):
            ct_copy(k).start()
        cp_g.wait()
        for g in range(8):
            h_copy(g, 0).start()

    def ct_first(k):
        ct_copy(k).wait_recv()
        ct_copy(3 + k).start()
        ct_copy(5 + k).start()

    def ct_second():
        wait_bytes(ct.at[:, pl.ds(0, TOK)], ct_r.at[2])
        ct_copy(7).start()
        wait_bytes(ct.at[:, pl.ds(0, 4 * TOK)], ct_r.at[3])
        wait_bytes(hp.at[:, pl.ds(0, TOK)], own_sem.at[0])

    def xr_copy(g):
        return remote(part.at[g], xr.at[g], send_sem.at[5], xr_r.at[g], d_x)

    def zr_copy(m):
        up = m % 2 == 0
        if m < 2:
            return remote(part.at[5 + m], zr.at[m], send_sem.at[6], zr_r.at[m], d_z[1 if up else 3])
        rows = pl.ds((m - 2) * (KV // 2), KV // 2)
        return remote(part.at[4, rows], zf.at[m - 2], send_sem.at[6], zr_r.at[m], d_z[1 if up else 3])

    def grad(g):
        wait_bytes(hp.at[g, pl.ds(TOK, 7 * TOK)], h_r.at[g])
        if g >= 4:
            xr_copy(g - 4).wait_recv()
        if g in (5, 6):
            zr_copy(g - 3).wait_recv()
        for q in range(4):
            rows = slice(q * 256, (q + 1) * 256)
            t = jnp.dot(ct[rows, :], hp[g], preferred_element_type=F32) * FACTOR
            if g >= 4:
                t = t + xr[g - 4, rows, :].astype(F32)
            if g in (5, 6) and q // 2 == g - 5:
                t = t + zf[g - 5, (q % 2) * 256:(q % 2 + 1) * 256, :].astype(F32)
            part[g, rows, :] = t.astype(BF16)
        if g < 4:
            xr_copy(g).start()
        elif g == 4:
            zr_copy(2).start()
            zr_copy(3).start()
        elif g < 7:
            zr_copy(g - 5).start()

    d0 = pl.multiple_of(i * 512 + z * 128, 128)

    def grad_last():
        zr_copy(0).wait_recv()
        zr_copy(1).wait_recv()
        for q in range(4):
            rows = slice(q * 256, (q + 1) * 256)
            total = part[7, rows, :].astype(F32) + zr[0, rows, :].astype(F32) + zr[1, rows, :].astype(F32)
            total = total * gv[0:1, pl.ds(d0, 128)]
            wg_ref[0, :, rows] = jnp.transpose(total).astype(BF16)

    def w_q(kb, k):
        z_copy(kb, k).wait_recv()
        z_copy(kb, 2 + k).start()
        x_copy(kb, k).start()

    def w_p(kb, k):
        z_copy(kb, 4 + k).wait_recv()
        z_copy(kb, 6 + k).start()
        sib_copy(kb, k).start()

    def w_bq(kb):
        wait_bytes(wall.at[kb, 0, pl.ds(0, QR)], z_r.at[kb, 2])
        x_copy(kb, 2).start()

    def w_bp(kb):
        wait_bytes(wall.at[kb, 0, pl.ds(0, PR)], z_r.at[kb, 5])
        sib_copy(kb, 2).start()

    def w_c(kb):
        wait_bytes(wall.at[kb, pl.ds(0, 3), pl.ds(0, QR)], xw_r.at[kb])
        for k in range(3):
            sib_copy(kb, 3 + k).start()

    def pass_copy(kb):
        return remote(vst.at[kb], pass_ref.at[0, :, pl.ds(kb * KB, KB)], send_sem.at[7], v_r.at[0], d_sec)

    def h_block(zz, r):
        return hv[zz * 4 + r].astype(F32)

    def gain_block(zz, r):
        return gv[0:1, pl.ds(pl.multiple_of(zz * SHARD + r * BLK, BLK), BLK)]

    def normalize():
        @pl.loop(0, NZ)
        def _(zz):
            for r in range(4):
                nv[zz, :, r * BLK:(r + 1) * BLK] = (h_block(zz, r) * inv[:, 0:1] * gain_block(zz, r)).astype(BF16)

    def grad_of(kb, zz, lo, size):
        return lax.dot_general(cv[:, kb * KB:(kb + 1) * KB], wall[kb, zz, lo:lo + size, :], (((1,), (1,)), ((), ())),
                               preferred_element_type=F32)

    def w_d(kb):
        wait_bytes(wall.at[kb, pl.ds(0, 3), pl.ds(0, 1024)], sw_r.at[kb])
        cols = slice(kb * KB, (kb + 1) * KB)
        last = kb == NB - 1

        def step(zz, acc):
            if not last:
                for lo in (0, 1024):
                    t = grad_of(kb, zz, lo, 1024)
                    if kb == 0:
                        ng[zz, :, lo:lo + 1024] = t
                    else:
                        ng[zz, :, lo:lo + 1024] = ng[zz, :, lo:lo + 1024] + t
            return acc + jnp.dot(nv[zz], wall[kb, zz], preferred_element_type=F32)

        vals = lax.fori_loop(0, NZ, step, jnp.zeros((TOK, KB), F32))
        vst[kb] = vals.astype(BF16)
        pass_copy(kb).start()
        prod = vals * cv[:, cols].astype(F32)
        prod = prod[:, 0:128] + prod[:, 128:256]
        if kb == 0:
            cdv[...] = prod
        else:
            cdv[...] = cdv[...] + prod

    def w_e():
        kb = NB - 1
        iv = inv[:, 0:1]
        coef = iv * iv * (jnp.sum(cdv[...], axis=1, keepdims=True) * (1.0 / D))

        @pl.loop(0, NZ)
        def _(zz):
            for r in range(4):
                lanes = slice(r * BLK, (r + 1) * BLK)
                t = ng[zz, :, lanes] + grad_of(kb, zz, r * BLK, BLK)
                ig_ref[0, :, pl.ds(pl.multiple_of(zz * SHARD + r * BLK, BLK), BLK)] = (
                    iv * gain_block(zz, r) * t - h_block(zz, r) * coef).astype(BF16)

    h_send(0)
    scale_cot()
    h_send(1)
    dequant(0)
    dequant(1)
    dequant(2)
    p_send(0)
    w_q(0, 0)
    w_q(0, 1)
    normalize()
    w_q(1, 0)
    w_q(1, 1)
    w_q(2, 0)
    w_q(2, 1)
    w_q(3, 0)
    w_q(3, 1)
    dequant(3)
    w_p(0, 0)
    w_p(0, 1)
    w_bq(0)
    ct_first(0)
    ct_first(1)
    w_bq(1)
    p_send(1)
    h_send(2)
    h_send(3)
    p_send(2)
    h_send(4)
    w_bq(2)
    h_send(5)
    h_send(6)
    h_send(7)
    w_bq(3)
    w_bp(0)
    w_c(0)
    w_d(0)
    ct_second()
    w_p(1, 0)
    w_p(1, 1)
    w_c(1)
    w_c(2)
    grad(0)
    grad(1)
    grad(2)
    w_p(2, 0)
    w_p(2, 1)
    w_c(3)
    p_send(3)
    w_bp(1)
    grad(3)
    w_d(1)
    w_bp(2)
    grad(4)
    w_d(2)
    w_p(3, 0)
    w_p(3, 1)
    grad(5)
    w_bp(3)
    grad(6)
    w_d(3)
    w_e()
    grad(7)
    grad_last()
    wait_bytes(pass_ref, v_r.at[0])
    wait_bytes(hp.at[:, pl.ds(0, 7 * TOK)], send_sem.at[0])
    wait_bytes(ct.at[:, pl.ds(0, 7 * TOK)], send_sem.at[1])
    wait_bytes(wall.at[:, pl.ds(0, 3), pl.ds(0, PR + QR)], send_sem.at[2])
    wait_bytes(wall.at[:, pl.ds(0, 3), pl.ds(0, QR)], send_sem.at[3])
    wait_bytes(wall.at[:, pl.ds(0, 3), pl.ds(0, 1024)], send_sem.at[4])
    wait_bytes(part.at[pl.ds(0, 4)], send_sem.at[5])
    wait_bytes(part.at[pl.ds(4, 3)], send_sem.at[6])
    wait_bytes(vst, send_sem.at[7])


def hand_over(a_in, b_in, c_in, a_out, b_out, c_out, sem):
    copies = [pltpu.make_async_copy(a_in, a_out, sem.at[0]), pltpu.make_async_copy(c_in, c_out, sem.at[1])]
    for k in range(8):
        rows = pl.ds(k * 32, 32)
        copies.append(pltpu.make_async_copy(b_in.at[0, rows], b_out.at[0, rows], sem.at[2 + k]))
    for copy in copies:
        copy.start()
    for copy in copies:
        copy.wait()


def on_device(hidden_in, norm_gain, weight_codes, block_scales, value_grad):
    dma, any_ = pltpu.SemaphoreType.DMA, pl.BlockSpec(memory_space=pl.ANY)
    v = pltpu.VMEM
    out = pl.pallas_call(
        kernel,
        out_shape=(v((1, TOK, KV), BF16), v((1, TOK, D), BF16), v((1, 128, KV), BF16)),
        in_specs=[any_] * 5,
        out_specs=[pl.BlockSpec(memory_space=v)] * 3,
        scratch_shapes=[
            v((NBLK, TOK, BLK), BF16),
            v((TOK, KV), BF16),
            v((KV, 8 * TOK), BF16),
            v((NZ, TOK, SHARD), BF16),
            v((NB, NZ, SHARD, KB), BF16),
            v((2, SHARD, KB), jnp.int32),
            v((256, KV), jnp.int32),
            v((NZ, TOK, SHARD), F32),
            v((8, 8 * TOK, 128), BF16),
            v((8, KV, 128), BF16),
            v((4, KV, 128), BF16),
            v((2, KV, 128), BF16),
            v((2, KV // 2, 128), BF16),
            v((NB, TOK, KB), BF16),
            v((1, D), F32),
            v((8, KV), F32),
            v((TOK, 128), F32),
            v((TOK, 128), F32),
            dma((1,)), dma((4,)), dma((NB,)), dma((1,)), dma((8,)), dma((4,)), dma((NB, 6)), dma((NB,)), dma((NB,)),
            dma((4,)), dma((4,)), dma((1,)), dma((8,)),
        ],
        compiler_params=pltpu.CompilerParams(
            collective_id=0, has_side_effects=True, vmem_limit_bytes=57 * 2 ** 20),
        cost_estimate=pl.CostEstimate(flops=3 * 2 * TOK * D * KV, bytes_accessed=24 * 2 ** 20, transcendentals=TOK),
    )(hidden_in, norm_gain, weight_codes, block_scales, value_grad)
    return pl.pallas_call(
        hand_over,
        out_shape=tuple(jax.ShapeDtypeStruct(o.shape, o.dtype) for o in out),
        in_specs=[pl.BlockSpec(memory_space=v)] * 3,
        out_specs=[any_] * 3,
        scratch_shapes=[dma((10,))],
        compiler_params=pltpu.CompilerParams(vmem_limit_bytes=2 * 2 ** 20),
    )(*out)


def solution(mesh):
    return jax.shard_map(
        on_device,
        mesh=mesh,
        in_specs=(
            P("section", ("dp", "node"), None),
            P("section", None),
            P("section", "node", None),
            P("section", "node", None),
            P("section", ("dp", "node"), None),
        ),
        out_specs=(
            P("section", ("dp", "node"), None),
            P("section", ("dp", "node"), None),
            P("section", ("dp", "node"), None),
        ),
        check_vma=False,
    )
```

time: 86.8 us -> 80.7 us (0.930)
  Pallas kernels: 86.1 us -> 79.8 us
    pallas_call x1, Pallas kernels: 81.6 us -> 77.4 us  [on_device(): pl.pallas_call(kernel, out_shape=(v((1, TOK, KV), BF16), v((1, TOK, D), B...]
    pallas_call x1, Pallas kernels: 4.44 us -> 2.35 us  [on_device(): pl.pallas_call(hand_over, out_shape=tuple((jax.ShapeDtypeStruct(o.shape,...]
where the time goes in v4:
time: 80.7 us; the launch traced here: 80.6 us
  Pallas kernels  79.8 us (99%)
    pallas_call x1, Pallas kernels, on_device(): pl.pallas_call(kernel, out_shape=(v((1, TOK, KV), BF16), v((1, TOK, D), B...  77.4 us
    pallas_call x1, Pallas kernels, on_device(): pl.pallas_call(hand_over, out_shape=tuple((jax.ShapeDtypeStruct(o.shape,...  2.35 us

profile of v4, /device:TPU:1, one launch (start us, length us, event | category | flops | bytes accessed | tf_op | source)
XLA Modules:
  0.0 80.6 jit_solution(6767013419092982139)
XLA Ops:
  0.6 77.4 %shard_map.76 = (bf16[1,256,1024]{2,1,0:T(8,128)(2,1)S(1)}, bf16[1,256,8192]{2,1,0:T(8,128)(2,1)S(1)}, bf16[1,128,1024]{2,1,0:T(8,128)(2,1)S(1)}) custom-call(bf16[1,256,8192]{2,1,0:T(8,128)(2,1)} %h_ref.1, f32[1,8192]{1,0:T(1,128)} %gain_ref.1, s32[1,2048,1024]{2,1,0:T(8,128)} %codes_ref.1, f32[1,8,1024]{2,1,0:T(8,128)} %scales_ref.1, ...), custom_call_target="tpu_custom_call" | custom-call | flops 12884901888 | bytes 25165824 | tf_op jit(solution)/shard_map/pallas_call | solution.py:403
  78.1 2.3 %shard_map.77 = (bf16[1,256,1024]{2,1,0:T(8,128)(2,1)}, bf16[1,256,8192]{2,1,0:T(8,128)(2,1)}, bf16[1,128,1024]{2,1,0:T(8,128)(2,1)}) custom-call(bf16[1,256,1024]{2,1,0:T(8,128)(2,1)S(1)} %get-tuple-element.6.a_in, bf16[1,256,8192]{2,1,0:T(8,128)(2,1)S(1)} %get-tuple-element.7.b_in, bf16[1,128,1024]{2,1,0:T(8,128)(2,1)S(1)} %get-tuple-element.8.c_in), custom_call_target="tpu_custom_call" | custom-call | tf_op jit(solution)/shard_map/pallas_call | solution.py:434

commit v5 on v4

--- a/solution.py
+++ b/solution.py
@@ -77,7 +77,11 @@
         yy = y if slot < 2 else (yp, ym, yo)[slot // 2 - 1]
         cc = c if slot % 2 == 0 else 1 - c
         lanes = pl.ds(pl.multiple_of(((z + ORDER[g % 4]) % 4) * 128, 128), 128)
-        src, dst = hv.at[xx * 8 + yy * 2 + cc, :, lanes], hp.at[g, pl.ds(slot * TOK, TOK)]
+        b = xx * 8 + yy * 2 + cc
+        src, dst = hv.at[b, :, lanes], hp.at[g, pl.ds(slot * TOK, TOK)]
+        if g == 0 and slot:
+            col = b * BLK + ((z + ORDER[0]) % 4) * 128
+            src = h_ref.at[0, :, pl.ds(pl.multiple_of(col, 128), 128)]
         if slot == 0:
             return pltpu.make_async_copy(src, dst, own_sem.at[0])
         return remote(src, dst, send_sem.at[0], h_r.at[g],
@@ -148,19 +152,20 @@
         z_copy(kb, 4).start()
         z_copy(kb, 5).start()
 
+    pl.semaphore_wait(barrier, 11)
+    h_send(0)
     cp_q.wait()
     cp_s.wait()
     for kb in range(NB):
         cols = slice(kb * KB, (kb + 1) * KB)
         wall[kb, z, pl.ds(pl.multiple_of(quick * 256, 256), 256), :] = (
             cq[:, cols].astype(F32) * sv[pl.ds(quick, 1), cols]).astype(BF16)
-    pl.semaphore_wait(barrier, 11)
-    for kb in range(NB):
         z_copy(kb, 0).start()
         z_copy(kb, 1).start()
-    wait_bytes(hv, hl_sem.at[0])
 
     def scale_cot():
+        wait_bytes(hv, hl_sem.at[0])
+
         def squares(b, acc):
             v = hv[b].astype(F32)
             v = v * v
@@ -192,10 +197,11 @@
     def xr_copy(g):
         return remote(part.at[g], xr.at[g], send_sem.at[5], xr_r.at[g], d_x)
 
-    def zr_copy(m):
+    def zr_copy(m, half=0):
         up = m % 2 == 0
         if m < 2:
-            return remote(part.at[5 + m], zr.at[m], send_sem.at[6], zr_r.at[m], d_z[1 if up else 3])
+            rows = pl.ds(half * (KV // 2), KV // 2)
+            return remote(part.at[5 + m, rows], zr.at[m, rows], send_sem.at[6], zr_r.at[m], d_z[1 if up else 3])
         rows = pl.ds((m - 2) * (KV // 2), KV // 2)
         return remote(part.at[4, rows], zf.at[m - 2], send_sem.at[6], zr_r.at[m], d_z[1 if up else 3])
 
@@ -213,19 +219,19 @@
             if g in (5, 6) and q // 2 == g - 5:
                 t = t + zf[g - 5, (q % 2) * 256:(q % 2 + 1) * 256, :].astype(F32)
             part[g, rows, :] = t.astype(BF16)
+            if g in (5, 6) and q % 2:
+                zr_copy(g - 5, q // 2).start()
         if g < 4:
             xr_copy(g).start()
         elif g == 4:
             zr_copy(2).start()
             zr_copy(3).start()
-        elif g < 7:
-            zr_copy(g - 5).start()
 
     d0 = pl.multiple_of(i * 512 + z * 128, 128)
 
     def grad_last():
-        zr_copy(0).wait_recv()
-        zr_copy(1).wait_recv()
+        wait_bytes(zr.at[0], zr_r.at[0])
+        wait_bytes(zr.at[1], zr_r.at[1])
         for q in range(4):
             rows = slice(q * 256, (q + 1) * 256)
             total = part[7, rows, :].astype(F32) + zr[0, rows, :].astype(F32) + zr[1, rows, :].astype(F32)
@@ -312,56 +318,55 @@
                 ig_ref[0, :, pl.ds(pl.multiple_of(zz * SHARD + r * BLK, BLK), BLK)] = (
                     iv * gain_block(zz, r) * t - h_block(zz, r) * coef).astype(BF16)
 
-    h_send(0)
     scale_cot()
     h_send(1)
     dequant(0)
+    w_q(0, 0)
+    w_q(0, 1)
+    p_send(0)
+    normalize()
+    w_q(1, 1)
+    w_q(1, 0)
+    w_q(2, 1)
+    w_q(2, 0)
+    w_q(3, 1)
     dequant(1)
     dequant(2)
-    p_send(0)
-    w_q(0, 0)
-    w_q(0, 1)
-    normalize()
-    w_q(1, 0)
-    w_q(1, 1)
-    w_q(2, 0)
-    w_q(2, 1)
+    dequant(3)
+    w_bq(0)
     w_q(3, 0)
-    w_q(3, 1)
-    dequant(3)
+    ct_first(0)
+    ct_first(1)
+    h_send(2)
     w_p(0, 0)
     w_p(0, 1)
-    w_bq(0)
-    ct_first(0)
-    ct_first(1)
     w_bq(1)
-    p_send(1)
-    h_send(2)
     h_send(3)
-    p_send(2)
     h_send(4)
-    w_bq(2)
     h_send(5)
     h_send(6)
-    h_send(7)
+    w_bq(2)
     w_bq(3)
+    p_send(1)
+    p_send(2)
+    w_c(0)
     w_bp(0)
-    w_c(0)
     w_d(0)
     ct_second()
-    w_p(1, 0)
-    w_p(1, 1)
     w_c(1)
     w_c(2)
+    w_p(1, 1)
     grad(0)
+    w_c(3)
+    w_p(1, 0)
     grad(1)
     grad(2)
     w_p(2, 0)
     w_p(2, 1)
-    w_c(3)
+    h_send(7)
+    grad(3)
+    w_bp(1)
     p_send(3)
-    w_bp(1)
-    grad(3)
     w_d(1)
     w_bp(2)
     grad(4)
@@ -369,8 +374,8 @@
     w_p(3, 0)
     w_p(3, 1)
     grad(5)
+    grad(6)
     w_bp(3)
-    grad(6)
     w_d(3)
     w_e()
     grad(7)

time: 80.7 us -> 80.1 us (level)
  Pallas kernels: 79.8 us -> 78.5 us
    pallas_call x1, Pallas kernels: 77.4 us -> 76.1 us  [on_device(): pl.pallas_call(kernel, out_shape=(v((1, TOK, KV), BF16), v((1, TOK, D), B...]
where the time goes in v5:
time: 80.1 us; the launch traced here: 79.3 us
  Pallas kernels  78.5 us (98%)
    pallas_call x1, Pallas kernels, on_device(): pl.pallas_call(kernel, out_shape=(v((1, TOK, KV), BF16), v((1, TOK, D), B...  76.1 us
    pallas_call x1, Pallas kernels, on_device(): pl.pallas_call(hand_over, out_shape=tuple((jax.ShapeDtypeStruct(o.shape,...  2.35 us

profile of v5, /device:TPU:1, one launch (start us, length us, event | category | flops | bytes accessed | tf_op | source)
XLA Modules:
  0.0 79.3 jit_solution(14537792861136503723)
XLA Ops:
  0.6 76.1 %shard_map.76 = (bf16[1,256,1024]{2,1,0:T(8,128)(2,1)S(1)}, bf16[1,256,8192]{2,1,0:T(8,128)(2,1)S(1)}, bf16[1,128,1024]{2,1,0:T(8,128)(2,1)S(1)}) custom-call(bf16[1,256,8192]{2,1,0:T(8,128)(2,1)} %h_ref.1, f32[1,8192]{1,0:T(1,128)} %gain_ref.1, s32[1,2048,1024]{2,1,0:T(8,128)} %codes_ref.1, f32[1,8,1024]{2,1,0:T(8,128)} %scales_ref.1, ...), custom_call_target="tpu_custom_call" | custom-call | flops 12884901888 | bytes 25165824 | tf_op jit(solution)/shard_map/pallas_call | solution.py:408
  76.8 2.3 %shard_map.77 = (bf16[1,256,1024]{2,1,0:T(8,128)(2,1)}, bf16[1,256,8192]{2,1,0:T(8,128)(2,1)}, bf16[1,128,1024]{2,1,0:T(8,128)(2,1)}) custom-call(bf16[1,256,1024]{2,1,0:T(8,128)(2,1)S(1)} %get-tuple-element.6.a_in, bf16[1,256,8192]{2,1,0:T(8,128)(2,1)S(1)} %get-tuple-element.7.b_in, bf16[1,128,1024]{2,1,0:T(8,128)(2,1)S(1)} %get-tuple-element.8.c_in), custom_call_target="tpu_custom_call" | custom-call | tf_op jit(solution)/shard_map/pallas_call | solution.py:439

commit v6 on v5

--- a/solution.py
+++ b/solution.py
@@ -16,13 +16,15 @@
 BLK = 512
 NBLK = D // BLK
 FACTOR = 2.0 ** -7
-QR = 208
+QR = (192, 192, 192, 192)
 ORDER = (2, 1, 3, 0)
-PR = 1024 - 2 * QR
+FIRST = 5 * TOK
+PR = tuple(1024 - 2 * q for q in QR)
+Q_MEAN = sum(QR) // NB
 
 
 def kernel(h_ref, gain_ref, codes_ref, scales_ref, cot_ref, pass_ref, ig_ref, wg_ref,
-           hv, cv, ct, nv, wall, cod, cq, ng, hp, part, xr, zr, zf, vst, gv, sv, inv, cdv,
+           hv, cv, ct, nv, wall, cod, cq, ng, hp, part, xr, zr, zf, first, vst, gv, sv, inv, cdv, vals,
            hl_sem, l_sem, cod_sem, own_sem, h_r, ct_r, z_r, xw_r, sw_r, xr_r, zr_r, v_r, send_sem):
     sec, i, z = lax.axis_index("section"), lax.axis_index("dp"), lax.axis_index("node")
     x, y, c = i // 8, (i // 2) % 4, i % 2
@@ -74,8 +76,8 @@
 
     def h_copy(g, slot):
         xx = (x + 1 + g // 4) % 2
-        yy = y if slot < 2 else (yp, ym, yo)[slot // 2 - 1]
-        cc = c if slot % 2 == 0 else 1 - c
+        yy = y if slot < 2 else (yp, ym, yo)[(slot - 2) % 3]
+        cc = c if slot in (0, 2, 3, 4) else 1 - c
         lanes = pl.ds(pl.multiple_of(((z + ORDER[g % 4]) % 4) * 128, 128), 128)
         b = xx * 8 + yy * 2 + cc
         src, dst = hv.at[b, :, lanes], hp.at[g, pl.ds(slot * TOK, TOK)]
@@ -84,11 +86,11 @@
             src = h_ref.at[0, :, pl.ds(pl.multiple_of(col, 128), 128)]
         if slot == 0:
             return pltpu.make_async_copy(src, dst, own_sem.at[0])
-        return remote(src, dst, send_sem.at[0], h_r.at[g],
-                      d_sib if slot == 1 else d_y[slot // 2 - 1, slot % 2])
+        return remote(src, dst, send_sem.at[0], h_r.at[8 if g == 7 and slot > 4 else g],
+                      d_sib if slot == 1 else d_y[(slot - 2) % 3, (slot - 2) // 3])
 
     def h_send(g):
-        for slot in (2, 4, 6, 3, 5, 7, 1):
+        for slot in (2, 3, 4, 1, 5, 6, 7):
             h_copy(g, slot).start()
 
     def ct_copy(k):
@@ -96,23 +98,25 @@
             return pl.ds(slot * TOK, TOK)
 
         if k < 3:
-            src, dst, target = ct.at[:, cols(0)], ct.at[:, cols((2, 4, 1)[k])], (d_y[0, 0], d_y[1, 0], d_sib)[k]
+            src, dst, target = ct.at[:, cols(0)], ct.at[:, cols((2, 3, 1)[k])], (d_y[0, 0], d_y[1, 0], d_sib)[k]
         elif k < 5:
             rows = pl.ds((k - 3) * (KV // 2), KV // 2)
-            src, dst, target = ct.at[rows, cols((2, 4)[k - 3])], ct.at[rows, cols(6)], d_y[k - 3, 0]
+            src, dst, target = ct.at[rows, cols((2, 3)[k - 3])], ct.at[rows, cols(4)], d_y[k - 3, 0]
         else:
-            slot = (2, 4, 6)[k - 5]
-            src, dst, target = ct.at[:, cols(slot)], ct.at[:, cols(slot + 1)], d_sib
+            slot = (2, 3, 4)[k - 5]
+            src, dst, target = ct.at[:, cols(slot)], ct.at[:, cols(slot + 3)], d_sib
         return remote(src, dst, send_sem.at[1], ct_r.at[(0, 1, 3, 2, 2, 3, 3, 3)[k]], target)
 
     base = c * 1024
-    p0 = pl.multiple_of(base + QR, 16)
-    q0 = pl.multiple_of(base + x * (QR + PR), 16)
-    q1 = pl.multiple_of(base + (1 - x) * (QR + PR), 16)
-    r0 = pl.multiple_of(base + x * QR, 16)
+
+    def row(offset):
+        return pl.multiple_of(base + offset, 16)
 
     def z_copy(kb, k):
-        start, size = (q0, QR) if k < 4 else (p0, PR)
+        if k < 4:
+            start, size = row(x * (QR[kb] + PR[kb])), QR[kb]
+        else:
+            start, size = row(QR[kb]), PR[kb]
         half = (size + 31) // 32 * 16
         if k % 4 < 2:
             ref = wall.at[kb, z, pl.ds(start, size)]
@@ -125,15 +129,15 @@
     shards = (zm, zp, z2)
 
     def x_copy(kb, k):
-        ref = wall.at[kb, shards[k], pl.ds(q0, QR)]
+        ref = wall.at[kb, shards[k], pl.ds(row(x * (QR[kb] + PR[kb])), QR[kb])]
         return remote(ref, ref, send_sem.at[3], xw_r.at[kb], d_x)
 
     def sib_copy(kb, k):
         if k < 3:
-            ref = wall.at[kb, shards[k], pl.ds(r0, PR + QR)]
+            ref = wall.at[kb, shards[k], pl.ds(row(x * QR[kb]), PR[kb] + QR[kb])]
         else:
-            ref = wall.at[kb, shards[k - 3], pl.ds(q1, QR)]
-        return remote(ref, ref, send_sem.at[4], sw_r.at[kb], d_sib)
+            ref = wall.at[kb, shards[k - 3], pl.ds(row((1 - x) * (QR[kb] + PR[kb])), QR[kb])]
+        return remote(ref, ref, send_sem.at[4], sw_r.at[kb, 1 if k == 2 else 0], d_sib)
 
     def dequant(kb):
         load_codes(kb).wait()
@@ -205,15 +209,25 @@
         rows = pl.ds((m - 2) * (KV // 2), KV // 2)
         return remote(part.at[4, rows], zf.at[m - 2], send_sem.at[6], zr_r.at[m], d_z[1 if up else 3])
 
+    def grad_first():
+        wait_bytes(hp.at[7, pl.ds(TOK, 4 * TOK)], h_r.at[7])
+        for q in range(4):
+            rows = slice(q * 256, (q + 1) * 256)
+            first[rows, :] = jnp.dot(ct[rows, :FIRST], hp[7, :FIRST, :], preferred_element_type=F32)
+
     def grad(g):
-        wait_bytes(hp.at[g, pl.ds(TOK, 7 * TOK)], h_r.at[g])
+        wait_bytes(hp.at[g, pl.ds(TOK, (3 if g == 7 else 7) * TOK)], h_r.at[8 if g == 7 else g])
         if g >= 4:
             xr_copy(g - 4).wait_recv()
         if g in (5, 6):
             zr_copy(g - 3).wait_recv()
         for q in range(4):
             rows = slice(q * 256, (q + 1) * 256)
-            t = jnp.dot(ct[rows, :], hp[g], preferred_element_type=F32) * FACTOR
+            if g == 7:
+                t = jnp.dot(ct[rows, FIRST:], hp[g, FIRST:, :], preferred_element_type=F32)
+                t = (t + first[rows, :]) * FACTOR
+            else:
+                t = jnp.dot(ct[rows, :], hp[g], preferred_element_type=F32) * FACTOR
             if g >= 4:
                 t = t + xr[g - 4, rows, :].astype(F32)
             if g in (5, 6) and q // 2 == g - 5:
@@ -249,15 +263,15 @@
         sib_copy(kb, k).start()
 
     def w_bq(kb):
-        wait_bytes(wall.at[kb, 0, pl.ds(0, QR)], z_r.at[kb, 2])
+        wait_bytes(wall.at[kb, 0, pl.ds(0, QR[kb])], z_r.at[kb, 2])
         x_copy(kb, 2).start()
 
     def w_bp(kb):
-        wait_bytes(wall.at[kb, 0, pl.ds(0, PR)], z_r.at[kb, 5])
+        wait_bytes(wall.at[kb, 0, pl.ds(0, PR[kb])], z_r.at[kb, 5])
         sib_copy(kb, 2).start()
 
     def w_c(kb):
-        wait_bytes(wall.at[kb, pl.ds(0, 3), pl.ds(0, QR)], xw_r.at[kb])
+        wait_bytes(wall.at[kb, pl.ds(0, 3), pl.ds(0, QR[kb])], xw_r.at[kb])
         for k in range(3):
             sib_copy(kb, 3 + k).start()
 
@@ -280,111 +294,141 @@
         return lax.dot_general(cv[:, kb * KB:(kb + 1) * KB], wall[kb, zz, lo:lo + size, :], (((1,), (1,)), ((), ())),
                                preferred_element_type=F32)
 
-    def w_d(kb):
-        wait_bytes(wall.at[kb, pl.ds(0, 3), pl.ds(0, 1024)], sw_r.at[kb])
-        cols = slice(kb * KB, (kb + 1) * KB)
-        last = kb == NB - 1
-
-        def step(zz, acc):
-            if not last:
-                for lo in (0, 1024):
-                    t = grad_of(kb, zz, lo, 1024)
-                    if kb == 0:
-                        ng[zz, :, lo:lo + 1024] = t
-                    else:
-                        ng[zz, :, lo:lo + 1024] = ng[zz, :, lo:lo + 1024] + t
-            return acc + jnp.dot(nv[zz], wall[kb, zz], preferred_element_type=F32)
-
-        vals = lax.fori_loop(0, NZ, step, jnp.zeros((TOK, KB), F32))
+    def near(kb):
+        wait_bytes(wall.at[kb, pl.ds(0, 2), pl.ds(0, 1024 + QR[kb] // 2)], sw_r.at[kb, 0])
+
+    def far(kb):
+        wait_bytes(wall.at[kb, 0, pl.ds(0, PR[kb] + QR[kb])], sw_r.at[kb, 1])
+
+    def add_grad(kb, zz):
+        for lo in (0, 1024):
+            t = grad_of(kb, zz, lo, 1024)
+            if kb == 0:
+                ng[zz, :, lo:lo + 1024] = t
+            else:
+                ng[zz, :, lo:lo + 1024] = ng[zz, :, lo:lo + 1024] + t
+
+    def finish(kb, vals):
         vst[kb] = vals.astype(BF16)
         pass_copy(kb).start()
-        prod = vals * cv[:, cols].astype(F32)
+        prod = vals * cv[:, kb * KB:(kb + 1) * KB].astype(F32)
         prod = prod[:, 0:128] + prod[:, 128:256]
         if kb == 0:
             cdv[...] = prod
         else:
             cdv[...] = cdv[...] + prod
 
-    def w_e():
+    def w_d(kb):
+        near(kb)
+        far(kb)
+
+        def step(zz, acc):
+            add_grad(kb, zz)
+            return acc + jnp.dot(nv[zz], wall[kb, zz], preferred_element_type=F32)
+
+        finish(kb, lax.fori_loop(0, NZ, step, jnp.zeros((TOK, KB), F32)))
+
+    def w_near():
         kb = NB - 1
+        near(kb)
+
+        def step(t, acc):
+            zz = (z + t + t // 2) % NZ
+            add_grad(kb, zz)
+            return acc + jnp.dot(nv[zz], wall[kb, zz], preferred_element_type=F32)
+
+        vals[...] = lax.fori_loop(0, 3, step, jnp.zeros((TOK, KB), F32))
+
+    def w_far():
+        kb = NB - 1
+        far(kb)
+        finish(kb, vals[...] + jnp.dot(nv[z2], wall[kb, z2], preferred_element_type=F32))
         iv = inv[:, 0:1]
         coef = iv * iv * (jnp.sum(cdv[...], axis=1, keepdims=True) * (1.0 / D))
-
-        @pl.loop(0, NZ)
-        def _(zz):
-            for r in range(4):
-                lanes = slice(r * BLK, (r + 1) * BLK)
-                t = ng[zz, :, lanes] + grad_of(kb, zz, r * BLK, BLK)
-                ig_ref[0, :, pl.ds(pl.multiple_of(zz * SHARD + r * BLK, BLK), BLK)] = (
-                    iv * gain_block(zz, r) * t - h_block(zz, r) * coef).astype(BF16)
+        cdv[...] = jnp.broadcast_to(coef, (TOK, 128))
+
+    def w_e(t):
+        zz = (z + (2, 0, 1, 3)[t]) % NZ
+        if t == 0:
+            add_grad(NB - 1, zz)
+        iv, coef = inv[:, 0:1], cdv[:, 0:1]
+        for r in range(4):
+            t_all = iv * gain_block(zz, r) * ng[zz, :, r * BLK:(r + 1) * BLK]
+            ig_ref[0, :, pl.ds(pl.multiple_of(zz * SHARD + r * BLK, BLK), BLK)] = (
+                t_all - h_block(zz, r) * coef).astype(BF16)
 
     scale_cot()
+    dequant(0)
+    p_send(0)
+    dequant(1)
     h_send(1)
-    dequant(0)
     w_q(0, 0)
     w_q(0, 1)
-    p_send(0)
-    normalize()
     w_q(1, 1)
     w_q(1, 0)
+    w_q(2, 0)
     w_q(2, 1)
-    w_q(2, 0)
+    dequant(2)
+    w_q(3, 0)
     w_q(3, 1)
-    dequant(1)
-    dequant(2)
-    dequant(3)
-    w_bq(0)
-    w_q(3, 0)
+    w_p(0, 1)
+    w_p(0, 0)
+    p_send(1)
     ct_first(0)
     ct_first(1)
     h_send(2)
-    w_p(0, 0)
-    w_p(0, 1)
+    w_bq(0)
     w_bq(1)
+    w_bq(2)
+    w_bq(3)
+    normalize()
+    w_c(0)
+    p_send(2)
+    w_bp(0)
     h_send(3)
+    w_d(0)
+    w_c(2)
+    ct_second()
+    w_c(1)
+    w_c(3)
+    w_p(1, 0)
+    w_p(1, 1)
+    grad(0)
+    grad(1)
+    grad(2)
     h_send(4)
     h_send(5)
-    h_send(6)
-    w_bq(2)
-    w_bq(3)
-    p_send(1)
-    p_send(2)
-    w_c(0)
-    w_bp(0)
-    w_d(0)
-    ct_second()
-    w_c(1)
-    w_c(2)
-    w_p(1, 1)
-    grad(0)
-    w_c(3)
-    w_p(1, 0)
-    grad(1)
-    grad(2)
     w_p(2, 0)
     w_p(2, 1)
+    dequant(3)
+    p_send(3)
+    h_send(6)
     h_send(7)
     grad(3)
     w_bp(1)
-    p_send(3)
     w_d(1)
+    grad(4)
     w_bp(2)
-    grad(4)
     w_d(2)
     w_p(3, 0)
     w_p(3, 1)
     grad(5)
+    w_near()
     grad(6)
     w_bp(3)
-    w_d(3)
-    w_e()
+    grad_first()
+    w_far()
+    w_e(3)
+    w_e(1)
+    w_e(0)
     grad(7)
+    w_e(2)
     grad_last()
     wait_bytes(pass_ref, v_r.at[0])
     wait_bytes(hp.at[:, pl.ds(0, 7 * TOK)], send_sem.at[0])
     wait_bytes(ct.at[:, pl.ds(0, 7 * TOK)], send_sem.at[1])
-    wait_bytes(wall.at[:, pl.ds(0, 3), pl.ds(0, PR + QR)], send_sem.at[2])
-    wait_bytes(wall.at[:, pl.ds(0, 3), pl.ds(0, QR)], send_sem.at[3])
+    wait_bytes(wall.at[:, pl.ds(0, 3), pl.ds(0, 1024 - Q_MEAN)], send_sem.at[2])
+    wait_bytes(wall.at[:, pl.ds(0, 3), pl.ds(0, Q_MEAN)], send_sem.at[3])
     wait_bytes(wall.at[:, pl.ds(0, 3), pl.ds(0, 1024)], send_sem.at[4])
     wait_bytes(part.at[pl.ds(0, 4)], send_sem.at[5])
     wait_bytes(part.at[pl.ds(4, 3)], send_sem.at[6])
@@ -424,12 +468,14 @@
             v((4, KV, 128), BF16),
             v((2, KV, 128), BF16),
             v((2, KV // 2, 128), BF16),
+            v((KV, 128), F32),
             v((NB, TOK, KB), BF16),
             v((1, D), F32),
             v((8, KV), F32),
             v((TOK, 128), F32),
             v((TOK, 128), F32),
-            dma((1,)), dma((4,)), dma((NB,)), dma((1,)), dma((8,)), dma((4,)), dma((NB, 6)), dma((NB,)), dma((NB,)),
+            v((TOK, KB), F32),
+            dma((1,)), dma((4,)), dma((NB,)), dma((1,)), dma((9,)), dma((4,)), dma((NB, 6)), dma((NB,)), dma((NB, 2)),
             dma((4,)), dma((4,)), dma((1,)), dma((8,)),
         ],
         compiler_params=pltpu.CompilerParams(

time: 80.1 us -> 81.9 us (1.022)
  Pallas kernels: 78.5 us -> 81 us
    pallas_call x1, Pallas kernels: 76.1 us -> 78.7 us  [on_device(): pl.pallas_call(kernel, out_shape=(v((1, TOK, KV), BF16), v((1, TOK, D), B...]
where the time goes in v6:
time: 81.9 us; the launch traced here: 81.8 us
  Pallas kernels  81 us (99%)
    pallas_call x1, Pallas kernels, on_device(): pl.pallas_call(kernel, out_shape=(v((1, TOK, KV), BF16), v((1, TOK, D), B...  78.7 us
    pallas_call x1, Pallas kernels, on_device(): pl.pallas_call(hand_over, out_shape=tuple((jax.ShapeDtypeStruct(o.shape,...  2.35 us

profile of v6, /device:TPU:1, one launch (start us, length us, event | category | flops | bytes accessed | tf_op | source)
XLA Modules:
  0.0 81.8 jit_solution(7009401201418053348)
XLA Ops:
  0.6 78.7 %shard_map.76 = (bf16[1,256,1024]{2,1,0:T(8,128)(2,1)S(1)}, bf16[1,256,8192]{2,1,0:T(8,128)(2,1)S(1)}, bf16[1,128,1024]{2,1,0:T(8,128)(2,1)S(1)}) custom-call(bf16[1,256,8192]{2,1,0:T(8,128)(2,1)} %h_ref.1, f32[1,8192]{1,0:T(1,128)} %gain_ref.1, s32[1,2048,1024]{2,1,0:T(8,128)} %codes_ref.1, f32[1,8,1024]{2,1,0:T(8,128)} %scales_ref.1, ...), custom_call_target="tpu_custom_call" | custom-call | flops 12884901888 | bytes 25165824 | tf_op jit(solution)/shard_map/pallas_call | solution.py:452
  79.3 2.3 %shard_map.77 = (bf16[1,256,1024]{2,1,0:T(8,128)(2,1)}, bf16[1,256,8192]{2,1,0:T(8,128)(2,1)}, bf16[1,128,1024]{2,1,0:T(8,128)(2,1)}) custom-call(bf16[1,256,1024]{2,1,0:T(8,128)(2,1)S(1)} %get-tuple-element.6.a_in, bf16[1,256,8192]{2,1,0:T(8,128)(2,1)S(1)} %get-tuple-element.7.b_in, bf16[1,128,1024]{2,1,0:T(8,128)(2,1)S(1)} %get-tuple-element.8.c_in), custom_call_target="tpu_custom_call" | custom-call | tf_op jit(solution)/shard_map/pallas_call | solution.py:485
